TPU v7x, 32 devices: a whole 2x2x4 slice. The times are simulated.
32 devices in a mesh: box: 8 (over z, core), agg: 4 (over y, x).
Axes of the slice: x: 2, y: 2, z: 4, core: 2. Of those that a mesh axis runs over, the one named last changes fastest.
Arguments:
- source: float32 [256, 128, 128], P('box', 'agg'), may hold values from -6 to 6
- guess: float32 [256, 128, 128], P('box', 'agg'), may hold values from -6 to 6
- reaction: float32 [256, 128, 128], P('box', 'agg'), may hold values from 0.001 to 0.02
- flags: int32 [8, 4, 4], P('box', 'agg'), may hold values from 0 to 1, as said below
Outputs:
- iterate: float32 [256, 128, 128], P('box', 'agg')
- level_one: float32 [128, 64, 64], P('box', 'agg')
- level_two: float32 [64, 32, 32], P('box', 'agg')
- level_three: float32 [32, 16, 16], P('box', 'agg')
- level_four: float32 [16, 8, 8], P('box', 'agg')
- bottom_residual: float32 [16, 8, 8], P('box', 'agg')
Inputs may be any that keep to these rules, and one draw needn't show every extreme that they name: `flags`: flags are 0 or 1; the share of refined boxes differs from device block to device block, and some blocks have none.
All inputs are finite; a program needn't handle non-finite values.
Results may differ from a plain program's by a relative error of at most 0.00018.
Values sent between devices are 32-bit elements; how exact they have to be, the bound alone decides.
A program may use at most 128 MiB of HBM per device.

v0:
```python
import jax
import jax.numpy as jnp
from jax import lax
from jax.sharding import PartitionSpec as P

LEVELS = 4


def passed_along(block, axis, distance):
    devices = range(lax.axis_size(axis))
    route = [(i - distance, i) for i in devices if i - distance in devices]
    return lax.ppermute(block, axis, route)


def extended(block, sides, width):
    for axis, dim in sides:
        count = lax.axis_size(axis)
        forward = [(i, i + 1) for i in range(count - 1)]
        backward = [(target, source) for source, target in forward]
        low = lax.ppermute(
            lax.slice_in_dim(block, block.shape[dim] - width, None, axis=dim), axis, forward
        )
        high = lax.ppermute(lax.slice_in_dim(block, 0, width, axis=dim), axis, backward)
        block = jnp.concatenate([low, block, high], axis=dim)
    return block


def swapped(block, axis, bit):
    count = lax.axis_size(axis)
    route = []
    for low in range(count):
        high = low | 1 << bit
        if high != low and high < count:
            route += [(low, high), (high, low)]
    return lax.ppermute(block, axis, route)


def neighbours(padded):
    count_x = padded.shape[0] - 2
    count_y = padded.shape[1] - 2
    count_z = padded.shape[2] - 2
    face_sum = jnp.zeros((count_x, count_y, count_z), jnp.float32)
    edge_sum = jnp.zeros((count_x, count_y, count_z), jnp.float32)
    corner_sum = jnp.zeros((count_x, count_y, count_z), jnp.float32)
    for step_x in (-1, 0, 1):
        for step_y in (-1, 0, 1):
            for step_z in (-1, 0, 1):
                moved = abs(step_x) + abs(step_y) + abs(step_z)
                if moved == 0:
                    continue
                window = padded[
                    1 + step_x : 1 + step_x + count_x,
                    1 + step_y : 1 + step_y + count_y,
                    1 + step_z : 1 + step_z + count_z,
                ]
                if moved == 1:
                    face_sum = face_sum + window
                elif moved == 2:
                    edge_sum = edge_sum + window
                else:
                    corner_sum = corner_sum + window
    return (face_sum + 0.5 * edge_sum + 0.25 * corner_sum) / 14.0


def padded_field(values, stride):
    top_plane = values[:, -1:, :]
    bottom_plane = values[:, :1, :]
    if stride < lax.axis_size("agg"):
        from_below = passed_along(top_plane, "agg", stride)
        from_above = passed_along(bottom_plane, "agg", -stride)
    else:
        from_below = jnp.zeros_like(top_plane)
        from_above = jnp.zeros_like(bottom_plane)
    padded_y = jnp.concatenate([from_below, values, from_above], axis=1)
    padded_xy = extended(padded_y, (("box", 0),), 1)
    return jnp.pad(padded_xy, ((0, 0), (0, 0), (1, 1)))


def operate(values, coefficient, stride):
    padded = padded_field(values, stride)
    return values - neighbours(padded) + coefficient * values


def restrict(values):
    size_a, size_b, size_c = values.shape
    return values.reshape(size_a // 2, 2, size_b // 2, 2, size_c // 2, 2).sum(axis=(1, 3, 5)) * 0.5


def cell_mask(flags, shape):
    boxes_x, boxes_y, boxes_z = flags.shape
    spread = jnp.broadcast_to(
        flags.astype(jnp.float32)[:, None, :, None, :, None],
        (boxes_x, shape[0] // boxes_x, boxes_y, shape[1] // boxes_y, boxes_z, shape[2] // boxes_z),
    )
    return spread.reshape(shape)


def coefficients(level_index):
    upper_edge = 1.1 * (2.0 + 0.02 * 4.0**level_index)
    lower_edge = upper_edge / 8.0
    midpoint = (upper_edge + lower_edge) / 2.0
    half_span = (upper_edge - lower_edge) / 2.0
    sigma_value = midpoint / half_span
    rho_first = 1.0 / sigma_value
    rho_second = 1.0 / (2.0 * sigma_value - rho_first)
    return (midpoint, rho_second * rho_first, 2.0 * rho_second / half_span)


def merge_pairs(coarse_source, coarse_reaction, stride, position):
    theirs_source, theirs_reaction = swapped(
        (coarse_source, coarse_reaction), "agg", stride.bit_length() - 1
    )
    upper_half = position // stride % 2 == 1
    merged_source = jnp.where(
        upper_half,
        jnp.concatenate([theirs_source, coarse_source], axis=1),
        jnp.concatenate([coarse_source, theirs_source], axis=1),
    )
    merged_reaction = jnp.where(
        upper_half,
        jnp.concatenate([theirs_reaction, coarse_reaction], axis=1),
        jnp.concatenate([coarse_reaction, theirs_reaction], axis=1),
    )
    return (merged_source, merged_reaction)


def per_device(source, guess, reaction, flags):
    agg_count = lax.axis_size("agg")
    position = lax.axis_index("agg")
    fine_rows = source.shape[1]
    refined = cell_mask(flags, source.shape)
    midpoint, factor_one, factor_two = coefficients(0)
    first_residual = refined * (source - operate(guess, reaction, 1))
    first_step = first_residual / midpoint
    current = guess + first_step
    mid_residual = refined * (source - operate(current, reaction, 1))
    second_step = factor_one * first_step + factor_two * mid_residual
    current = current + second_step
    residual = refined * (source - operate(current, reaction, 1))
    results = [current]
    coarse_reaction = reaction
    stride = 1
    extent = fine_rows
    for level_index in range(1, LEVELS + 1):
        coarse_source = restrict(residual)
        coarse_reaction = restrict(coarse_reaction)
        extent = extent // 2
        if stride < agg_count:
            coarse_source, coarse_reaction = merge_pairs(
                coarse_source, coarse_reaction, stride, position
            )
            stride = stride * 2
            extent = extent * 2
        midpoint, factor_one, factor_two = coefficients(level_index)
        first_step = coarse_source / midpoint
        mid_residual = coarse_source - operate(first_step, coarse_reaction, stride)
        second_step = factor_one * first_step + factor_two * mid_residual
        correction = first_step + second_step
        residual = coarse_source - operate(correction, coarse_reaction, stride)
        own_rows = fine_rows >> level_index
        local_start = position * own_rows - position // stride * extent
        results.append(lax.dynamic_slice_in_dim(correction, local_start, own_rows, 1))
        if level_index == LEVELS:
            bottom_residual = lax.dynamic_slice_in_dim(residual, local_start, own_rows, 1)
    return (results[0], results[1], results[2], results[3], results[4], bottom_residual)


def solution(mesh):
    in_specs = (
        P("box", "agg", None),
        P("box", "agg", None),
        P("box", "agg", None),
        P("box", "agg", None),
    )
    out_specs = (
        P("box", "agg", None),
        P("box", "agg", None),
        P("box", "agg", None),
        P("box", "agg", None),
        P("box", "agg", None),
        P("box", "agg", None),
    )
    return jax.shard_map(
        per_device, mesh=mesh, in_specs=in_specs, out_specs=out_specs, check_vma=False
    )
```

profile of v0, /device:TPU:1, one launch (start us, length us, event | category | flops | bytes accessed | tf_op | source)
XLA Modules:
  0.0 273.2 jit_solution(17601511418926221342)
XLA Ops:
  0.6 1.1 fusion.215
  1.7 3.9 %collective-permute-start = (f32[32,1,128]{2,1,0:T(1,128)S(1)}, f32[32,1,128]{2,1,0:T(1,128)S(1)}, u32[]{:S(2)}, u32[]{:S(2)}) collective-permute-start(f32[32,1,128]{2,1,0:T(1,128)S(1)} %get-tuple-element.26), channel_id=1, source_target_pairs={{0,1},{1,2},{2,3},{4,5},{5,6},{6,7},{8,9},{9,10},{10,11},{12,13},{... | collective-permute-start | bytes 49160 | tf_op jit(solution)/shard_map/ppermute | solution.py:12
  5.7 1.3 collective-permute-start.1
  7.0 3.2 %collective-permute-done.1 = f32[32,1,128]{2,1,0:T(1,128)S(1)} collective-permute-done((f32[32,1,128]{2,1,0:T(1,128)S(1)}, f32[32,1,128]{2,1,0:T(1,128)S(1)}, u32[]{:S(2)}, u32[]{:S(2)}) %collective-permute-start.1) | collective-permute-done | bytes 16416 | tf_op jit(solution)/shard_map/ppermute | solution.py:12
  10.9 5.2 %collective-permute-start.2 = (f32[1,34,128]{2,1,0:T(8,128)S(1)}, f32[1,34,128]{2,1,0:T(8,128)S(1)}, u32[]{:S(2)}, u32[]{:S(2)}) collective-permute-start(f32[1,34,128]{2,1,0:T(8,128)S(1)} %get-tuple-element.20), channel_id=1, source_target_pairs={{0,4},{4,8},{8,12},{12,16},{16,20},{20,24},{24,28},{1,5},{5,9},{9,... | collective-permute-start | bytes 52232 | tf_op jit(solution)/shard_map/ppermute | solution.py:20
  16.1 1.9 collective-permute-start.3
  18.8 2.4 collective-permute-done.3
  21.2 1.4 maximum_maximum_fusion
  23.8 1.4 multiply_add_fusion
  25.2 4.0 %collective-permute-start.4 = (f32[32,1,128]{2,1,0:T(1,128)S(1)}, f32[32,1,128]{2,1,0:T(1,128)S(1)}, u32[]{:S(2)}, u32[]{:S(2)}) collective-permute-start(f32[32,1,128]{2,1,0:T(1,128)S(1)} %get-tuple-element.24), channel_id=1, source_target_pairs={{0,1},{1,2},{2,3},{4,5},{5,6},{6,7},{8,9},{9,10},{10,11},{12,13},{... | collective-permute-start | bytes 49160 | tf_op jit(solution)/shard_map/ppermute | solution.py:12
  29.2 1.3 collective-permute-start.5
  30.6 3.2 %collective-permute-done.5 = f32[32,1,128]{2,1,0:T(1,128)S(1)} collective-permute-done((f32[32,1,128]{2,1,0:T(1,128)S(1)}, f32[32,1,128]{2,1,0:T(1,128)S(1)}, u32[]{:S(2)}, u32[]{:S(2)}) %collective-permute-start.5) | collective-permute-done | bytes 16416 | tf_op jit(solution)/shard_map/ppermute | solution.py:12
  33.7 3.4 %collective-permute-start.6 = (f32[1,34,128]{2,1,0:T(8,128)S(1)}, f32[1,34,128]{2,1,0:T(8,128)S(1)}, u32[]{:S(2)}, u32[]{:S(2)}) collective-permute-start(f32[1,34,128]{2,1,0:T(8,128)S(1)} %get-tuple-element.16), channel_id=1, source_target_pairs={{0,4},{4,8},{8,12},{12,16},{16,20},{20,24},{24,28},{1,5},{5,9},{9,... | collective-permute-start | bytes 52232 | tf_op jit(solution)/shard_map/ppermute | solution.py:20
  37.1 1.9 collective-permute-start.7
  39.0 3.2 %collective-permute-done.7 = f32[1,34,128]{2,1,0:T(8,128)S(1)} collective-permute-done((f32[1,34,128]{2,1,0:T(8,128)S(1)}, f32[1,34,128]{2,1,0:T(8,128)S(1)}, u32[]{:S(2)}, u32[]{:S(2)}) %collective-permute-start.7) | collective-permute-done | bytes 17440 | tf_op jit(solution)/shard_map/ppermute | solution.py:23
  42.9 1.4 fusion.21
  44.3 3.1 %collective-permute-start.8 = (f32[32,1,128]{2,1,0:T(1,128)S(1)}, f32[32,1,128]{2,1,0:T(1,128)S(1)}, u32[]{:S(2)}, u32[]{:S(2)}) collective-permute-start(f32[32,1,128]{2,1,0:T(1,128)S(1)} %get-tuple-element.22), channel_id=1, source_target_pairs={{0,1},{1,2},{2,3},{4,5},{5,6},{6,7},{8,9},{9,10},{10,11},{12,13},{... | collective-permute-start | bytes 49160 | tf_op jit(solution)/shard_map/ppermute | solution.py:12
  47.5 1.3 collective-permute-start.9
  48.8 3.2 %collective-permute-done.9 = f32[32,1,128]{2,1,0:T(1,128)S(1)} collective-permute-done((f32[32,1,128]{2,1,0:T(1,128)S(1)}, f32[32,1,128]{2,1,0:T(1,128)S(1)}, u32[]{:S(2)}, u32[]{:S(2)}) %collective-permute-start.9) | collective-permute-done | bytes 16416 | tf_op jit(solution)/shard_map/ppermute | solution.py:12
  52.0 3.4 %collective-permute-start.10 = (f32[1,34,128]{2,1,0:T(8,128)S(1)}, f32[1,34,128]{2,1,0:T(8,128)S(1)}, u32[]{:S(2)}, u32[]{:S(2)}) collective-permute-start(f32[1,34,128]{2,1,0:T(8,128)S(1)} %get-tuple-element.12), channel_id=1, source_target_pairs={{0,4},{4,8},{8,12},{12,16},{16,20},{20,24},{24,28},{1,5},{5,9},{9,... | collective-permute-start | bytes 52232 | tf_op jit(solution)/shard_map/ppermute | solution.py:20
  55.3 1.9 collective-permute-start.11
  57.3 3.2 %collective-permute-done.11 = f32[1,34,128]{2,1,0:T(8,128)S(1)} collective-permute-done((f32[1,34,128]{2,1,0:T(8,128)S(1)}, f32[1,34,128]{2,1,0:T(8,128)S(1)}, u32[]{:S(2)}, u32[]{:S(2)}) %collective-permute-start.11) | collective-permute-done | bytes 17440 | tf_op jit(solution)/shard_map/ppermute | solution.py:23
  61.1 1.4 fusion.7
  62.5 34.9 %reshape.46 = f32[16,2,16,2,64,2]{5,4,3,2,1,0:T(8,128)} reshape(f32[32,32,128]{2,1,0:T(8,128)S(1)} %fusion.7) | data formatting | bytes 1048576 | tf_op jit(solution)/shard_map/reshape | solution.py:86
  97.4 12.2 %reduce_sum.72 = f32[16,16,64]{2,1,0:T(8,128)S(1)} reduce(f32[16,2,16,2,64,2]{5,4,3,2,1,0:T(8,128)} %reshape.46, f32[]{:T(128)} %constant.115.clone.1), dimensions={1,3,5}, to_apply=%region_0.1 | reduce | flops 114688 | bytes 589828 | tf_op jit(solution)/shard_map/reduce_sum | solution.py:86
  110.3 3.2 %collective-permute-done.12 = f32[16,16,64]{2,1,0:T(8,128)S(1)} collective-permute-done((f32[16,16,64]{2,1,0:T(8,128)S(1)}, f32[16,16,64]{2,1,0:T(8,128)S(1)}, u32[]{:S(2)}, u32[]{:S(2)}) %collective-permute-start.12) | collective-permute-done | bytes 65568 | tf_op jit(solution)/shard_map/ppermute | solution.py:35
  113.6 1.3 collective-permute-start.13
  114.9 1.3 collective-permute-start.14
  116.2 34.9 %reshape.47 = f32[16,2,16,2,64,2]{5,4,3,2,1,0:T(8,128)} reshape(f32[32,32,128]{2,1,0:T(8,128)S(1)} %copy-done.2) | data formatting | bytes 1048576 | tf_op jit(solution)/shard_map/reshape | solution.py:86
  151.0 12.2 %reduce_sum.73 = f32[16,16,64]{2,1,0:T(8,128)S(1)} reduce(f32[16,2,16,2,64,2]{5,4,3,2,1,0:T(8,128)} %reshape.47, f32[]{:T(128)} %constant.115.clone.1), dimensions={1,3,5}, to_apply=%region_1.2 | reduce | flops 114688 | bytes 589828 | tf_op jit(solution)/shard_map/reduce_sum | solution.py:86
  163.3 3.8 %collective-permute-start.15 = (f32[1,34,64]{2,1,0:T(8,128)S(1)}, f32[1,34,64]{2,1,0:T(8,128)S(1)}, u32[]{:S(2)}, u32[]{:S(2)}) collective-permute-start(f32[1,34,64]{2,1,0:T(8,128)S(1)} %get-tuple-element.34), channel_id=1, source_target_pairs={{0,4},{4,8},{8,12},{12,16},{16,20},{20,24},{24,28},{1,5},{5,9},{9,... | collective-permute-start | bytes 26120 | tf_op jit(solution)/shard_map/ppermute | solution.py:20
  167.1 1.9 collective-permute-start.16
  169.8 2.5 collective-permute-done.16
  173.8 4.3 %collective-permute-start.18 = (f32[16,1,64]{2,1,0:T(1,128)S(1)}, f32[16,1,64]{2,1,0:T(1,128)S(1)}, u32[]{:S(2)}, u32[]{:S(2)}) collective-permute-start(f32[16,1,64]{2,1,0:T(1,128)S(1)} %get-tuple-element.36), channel_id=1, source_target_pairs={{0,2},{1,3},{4,6},{5,7},{8,10},{9,11},{12,14},{13,15},{16,18},{17,... | collective-permute-start | bytes 12296 | tf_op jit(solution)/shard_map/ppermute | solution.py:12
  178.0 1.3 collective-permute-start.19
  179.3 3.1 %collective-permute-done.19 = f32[16,1,64]{2,1,0:T(1,128)S(1)} collective-permute-done((f32[16,1,64]{2,1,0:T(1,128)S(1)}, f32[16,1,64]{2,1,0:T(1,128)S(1)}, u32[]{:S(2)}, u32[]{:S(2)}) %collective-permute-start.19) | collective-permute-done | bytes 4128 | tf_op jit(solution)/shard_map/ppermute | solution.py:12
  182.4 6.6 %collective-permute-start.20 = (f32[1,34,64]{2,1,0:T(8,128)S(1)}, f32[1,34,64]{2,1,0:T(8,128)S(1)}, u32[]{:S(2)}, u32[]{:S(2)}) collective-permute-start(f32[1,34,64]{2,1,0:T(8,128)S(1)} %get-tuple-element.30), channel_id=1, source_target_pairs={{0,4},{4,8},{8,12},{12,16},{16,20},{20,24},{24,28},{1,5},{5,9},{9,... | collective-permute-start | bytes 26120 | tf_op jit(solution)/shard_map/ppermute | solution.py:20
  189.1 1.9 collective-permute-start.21
  191.0 3.1 %collective-permute-done.21 = f32[1,34,64]{2,1,0:T(8,128)S(1)} collective-permute-done((f32[1,34,64]{2,1,0:T(8,128)S(1)}, f32[1,34,64]{2,1,0:T(8,128)S(1)}, u32[]{:S(2)}, u32[]{:S(2)}) %collective-permute-start.21) | collective-permute-done | bytes 8736 | tf_op jit(solution)/shard_map/ppermute | solution.py:23
  195.2 10.1 %reshape.48 = f32[8,2,16,2,32,2]{5,4,3,2,1,0:T(8,128)} reshape(f32[16,32,64]{2,1,0:T(8,128)S(1)} %fusion.43) | data formatting | bytes 262144 | tf_op jit(solution)/shard_map/reshape | solution.py:86
  205.3 4.1 %reduce_sum.74 = f32[8,16,32]{2,1,0:T(8,128)S(1)} reduce(f32[8,2,16,2,32,2]{5,4,3,2,1,0:T(8,128)} %reshape.48, f32[]{:T(128)} %constant.115.clone.1), dimensions={1,3,5}, to_apply=%region_2.3 | reduce | flops 28672 | bytes 147460 | tf_op jit(solution)/shard_map/reduce_sum | solution.py:86
  209.4 10.1 %select_n.76 = f32[8,2,16,2,32,2]{5,4,3,2,1,0:T(8,128)} reshape(f32[16,32,64]{2,1,0:T(8,128)S(1)} %maximum_select_fusion.1) | data formatting | bytes 262144 | tf_op jit(solution)/shard_map/jit(_where)/select_n | solution.py:119
  219.5 4.1 %reduce_sum.75 = f32[8,16,32]{2,1,0:T(8,128)S(1)} reduce(f32[8,2,16,2,32,2]{5,4,3,2,1,0:T(8,128)} %select_n.76, f32[]{:T(128)} %constant.115.clone.1), dimensions={1,3,5}, to_apply=%region_3.4 | reduce | flops 28672 | bytes 147460 | tf_op jit(solution)/shard_map/reduce_sum | solution.py:86
  223.7 1.9 collective-permute-start.23
  225.6 2.4 collective-permute-start.24
  228.0 1.5 collective-permute-start.25
  229.6 1.5 collective-permute-done.24
  232.6 3.6 %collective-permute-start.26 = (f32[1,34,32]{2,1,0:T(8,128)S(1)}, f32[1,34,32]{2,1,0:T(8,128)S(1)}, u32[]{:S(2)}, u32[]{:S(2)}) collective-permute-start(f32[1,34,32]{2,1,0:T(8,128)S(1)} %get-tuple-element.40), channel_id=1, source_target_pairs={{0,4},{4,8},{8,12},{12,16},{16,20},{20,24},{24,28},{1,5},{5,9},{9,... | collective-permute-start | bytes 13064 | tf_op jit(solution)/shard_map/ppermute | solution.py:20
  236.3 1.9 collective-permute-start.27
  238.3 3.1 %collective-permute-done.27 = f32[1,34,32]{2,1,0:T(8,128)S(1)} collective-permute-done((f32[1,34,32]{2,1,0:T(8,128)S(1)}, f32[1,34,32]{2,1,0:T(8,128)S(1)}, u32[]{:S(2)}, u32[]{:S(2)}) %collective-permute-start.27) | collective-permute-done | bytes 4384 | tf_op jit(solution)/shard_map/ppermute | solution.py:23
  242.2 1.1 reshape.49
  243.6 1.9 collective-permute-start.28
  245.5 2.4 collective-permute-start.29
  247.9 1.1 select_n.80
  249.3 1.2 collective-permute-done.29
  250.8 2.0 collective-permute-start.30
  252.8 2.4 collective-permute-start.31
  255.9 2.0 collective-permute-done.31
  258.4 1.9 collective-permute-start.32
  260.3 2.4 collective-permute-start.33
  263.6 1.7 collective-permute-done.33
  265.5 1.9 collective-permute-start.34
  267.5 2.4 collective-permute-start.35
  270.4 2.0 collective-permute-done.35
  (107 shorter events, 15.0 us)
Async XLA Ops:
  0.6 21.9 %copy-start.1 = (f32[32,32,128]{2,1,0:T(8,128)S(1)}, f32[32,32,128]{2,1,0:T(8,128)}, u32[]{:S(2)}) copy-start(f32[32,32,128]{2,1,0:T(8,128)} %param.5) | copy-start | bytes 1572868
  1.7 5.3 %collective-permute-start = (f32[32,1,128]{2,1,0:T(1,128)S(1)}, f32[32,1,128]{2,1,0:T(1,128)S(1)}, u32[]{:S(2)}, u32[]{:S(2)}) collective-permute-start(f32[32,1,128]{2,1,0:T(1,128)S(1)} %get-tuple-element.26), channel_id=1, source_target_pairs={{0,1},{1,2},{2,3},{4,5},{5,6},{6,7},{8,9},{9,10},{10,11},{12,13},{... | collective-permute-start | bytes 49160 | tf_op jit(solution)/shard_map/ppermute | solution.py:12
  5.7 4.5 %collective-permute-start.1 = (f32[32,1,128]{2,1,0:T(1,128)S(1)}, f32[32,1,128]{2,1,0:T(1,128)S(1)}, u32[]{:S(2)}, u32[]{:S(2)}) collective-permute-start(f32[32,1,128]{2,1,0:T(1,128)S(1)} %get-tuple-element.27), channel_id=1, source_target_pairs={{1,0},{2,1},{3,2},{5,4},{6,5},{7,6},{9,8},{10,9},{11,10},{13,12},{... | collective-permute-start | bytes 49160 | tf_op jit(solution)/shard_map/ppermute | solution.py:12
  10.9 7.9 %collective-permute-start.2 = (f32[1,34,128]{2,1,0:T(8,128)S(1)}, f32[1,34,128]{2,1,0:T(8,128)S(1)}, u32[]{:S(2)}, u32[]{:S(2)}) collective-permute-start(f32[1,34,128]{2,1,0:T(8,128)S(1)} %get-tuple-element.20), channel_id=1, source_target_pairs={{0,4},{4,8},{8,12},{12,16},{16,20},{20,24},{24,28},{1,5},{5,9},{9,... | collective-permute-start | bytes 52232 | tf_op jit(solution)/shard_map/ppermute | solution.py:20
  16.1 5.1 %collective-permute-start.3 = (f32[1,34,128]{2,1,0:T(8,128)S(1)}, f32[1,34,128]{2,1,0:T(8,128)S(1)}, u32[]{:S(2)}, u32[]{:S(2)}) collective-permute-start(f32[1,34,128]{2,1,0:T(8,128)S(1)} %get-tuple-element.21), channel_id=1, source_target_pairs={{4,0},{8,4},{12,8},{16,12},{20,16},{24,20},{28,24},{5,1},{9,5},{13... | collective-permute-start | bytes 52232 | tf_op jit(solution)/shard_map/ppermute | solution.py:23
  22.6 1.0 copy-start.2
  22.6 1.2 copy-start.3
  25.2 5.3 %collective-permute-start.4 = (f32[32,1,128]{2,1,0:T(1,128)S(1)}, f32[32,1,128]{2,1,0:T(1,128)S(1)}, u32[]{:S(2)}, u32[]{:S(2)}) collective-permute-start(f32[32,1,128]{2,1,0:T(1,128)S(1)} %get-tuple-element.24), channel_id=1, source_target_pairs={{0,1},{1,2},{2,3},{4,5},{5,6},{6,7},{8,9},{9,10},{10,11},{12,13},{... | collective-permute-start | bytes 49160 | tf_op jit(solution)/shard_map/ppermute | solution.py:12
  29.2 4.5 %collective-permute-start.5 = (f32[32,1,128]{2,1,0:T(1,128)S(1)}, f32[32,1,128]{2,1,0:T(1,128)S(1)}, u32[]{:S(2)}, u32[]{:S(2)}) collective-permute-start(f32[32,1,128]{2,1,0:T(1,128)S(1)} %get-tuple-element.25), channel_id=1, source_target_pairs={{1,0},{2,1},{3,2},{5,4},{6,5},{7,6},{9,8},{10,9},{11,10},{13,12},{... | collective-permute-start | bytes 49160 | tf_op jit(solution)/shard_map/ppermute | solution.py:12
  33.7 5.3 %collective-permute-start.6 = (f32[1,34,128]{2,1,0:T(8,128)S(1)}, f32[1,34,128]{2,1,0:T(8,128)S(1)}, u32[]{:S(2)}, u32[]{:S(2)}) collective-permute-start(f32[1,34,128]{2,1,0:T(8,128)S(1)} %get-tuple-element.16), channel_id=1, source_target_pairs={{0,4},{4,8},{8,12},{12,16},{16,20},{20,24},{24,28},{1,5},{5,9},{9,... | collective-permute-start | bytes 52232 | tf_op jit(solution)/shard_map/ppermute | solution.py:20
  37.1 5.1 %collective-permute-start.7 = (f32[1,34,128]{2,1,0:T(8,128)S(1)}, f32[1,34,128]{2,1,0:T(8,128)S(1)}, u32[]{:S(2)}, u32[]{:S(2)}) collective-permute-start(f32[1,34,128]{2,1,0:T(8,128)S(1)} %get-tuple-element.17), channel_id=1, source_target_pairs={{4,0},{8,4},{12,8},{16,12},{20,16},{24,20},{28,24},{5,1},{9,5},{13... | collective-permute-start | bytes 52232 | tf_op jit(solution)/shard_map/ppermute | solution.py:23
  44.3 16.8 %copy-start = (f32[32,32,128]{2,1,0:T(8,128)}, f32[32,32,128]{2,1,0:T(8,128)S(1)}, u32[]{:S(2)}) copy-start(f32[32,32,128]{2,1,0:T(8,128)S(1)} %fusion.21) | copy-start | bytes 1572868
  44.3 4.4 %collective-permute-start.8 = (f32[32,1,128]{2,1,0:T(1,128)S(1)}, f32[32,1,128]{2,1,0:T(1,128)S(1)}, u32[]{:S(2)}, u32[]{:S(2)}) collective-permute-start(f32[32,1,128]{2,1,0:T(1,128)S(1)} %get-tuple-element.22), channel_id=1, source_target_pairs={{0,1},{1,2},{2,3},{4,5},{5,6},{6,7},{8,9},{9,10},{10,11},{12,13},{... | collective-permute-start | bytes 49160 | tf_op jit(solution)/shard_map/ppermute | solution.py:12
  47.5 4.5 %collective-permute-start.9 = (f32[32,1,128]{2,1,0:T(1,128)S(1)}, f32[32,1,128]{2,1,0:T(1,128)S(1)}, u32[]{:S(2)}, u32[]{:S(2)}) collective-permute-start(f32[32,1,128]{2,1,0:T(1,128)S(1)} %get-tuple-element.23), channel_id=1, source_target_pairs={{1,0},{2,1},{3,2},{5,4},{6,5},{7,6},{9,8},{10,9},{11,10},{13,12},{... | collective-permute-start | bytes 49160 | tf_op jit(solution)/shard_map/ppermute | solution.py:12
  52.0 5.3 %collective-permute-start.10 = (f32[1,34,128]{2,1,0:T(8,128)S(1)}, f32[1,34,128]{2,1,0:T(8,128)S(1)}, u32[]{:S(2)}, u32[]{:S(2)}) collective-permute-start(f32[1,34,128]{2,1,0:T(8,128)S(1)} %get-tuple-element.12), channel_id=1, source_target_pairs={{0,4},{4,8},{8,12},{12,16},{16,20},{20,24},{24,28},{1,5},{5,9},{9,... | collective-permute-start | bytes 52232 | tf_op jit(solution)/shard_map/ppermute | solution.py:20
  55.3 5.1 %collective-permute-start.11 = (f32[1,34,128]{2,1,0:T(8,128)S(1)}, f32[1,34,128]{2,1,0:T(8,128)S(1)}, u32[]{:S(2)}, u32[]{:S(2)}) collective-permute-start(f32[1,34,128]{2,1,0:T(8,128)S(1)} %get-tuple-element.13), channel_id=1, source_target_pairs={{4,0},{8,4},{12,8},{16,12},{20,16},{24,20},{28,24},{5,1},{9,5},{13... | collective-permute-start | bytes 52232 | tf_op jit(solution)/shard_map/ppermute | solution.py:23
  109.6 3.9 %collective-permute-start.12 = (f32[16,16,64]{2,1,0:T(8,128)S(1)}, f32[16,16,64]{2,1,0:T(8,128)S(1)}, u32[]{:S(2)}, u32[]{:S(2)}) collective-permute-start(f32[16,16,64]{2,1,0:T(8,128)S(1)} %broadcast_multiply_fusion.3), channel_id=1, source_target_pairs={{0,1},{1,0},{2,3},{3,2},{4,5},{5,4},{6,7},{7,6},{8,9},{9,8},{10,11... | collective-permute-start | bytes 196616 | tf_op jit(solution)/shard_map/ppermute | solution.py:35
  113.6 49.7 %collective-permute-start.13 = (f32[16,1,64]{2,1,0:T(1,128)S(1)}, f32[16,1,64]{2,1,0:T(1,128)S(1)}, u32[]{:S(2)}, u32[]{:S(2)}) collective-permute-start(f32[16,1,64]{2,1,0:T(1,128)S(1)} %get-tuple-element.38), channel_id=1, source_target_pairs={{0,2},{1,3},{4,6},{5,7},{8,10},{9,11},{12,14},{13,15},{16,18},{17,... | collective-permute-start | bytes 12296 | tf_op jit(solution)/shard_map/ppermute | solution.py:12
  114.9 48.4 %collective-permute-start.14 = (f32[16,1,64]{2,1,0:T(1,128)S(1)}, f32[16,1,64]{2,1,0:T(1,128)S(1)}, u32[]{:S(2)}, u32[]{:S(2)}) collective-permute-start(f32[16,1,64]{2,1,0:T(1,128)S(1)} %get-tuple-element.39), channel_id=1, source_target_pairs={{2,0},{3,1},{6,4},{7,5},{10,8},{11,9},{14,12},{15,13},{18,16},{19,... | collective-permute-start | bytes 12296 | tf_op jit(solution)/shard_map/ppermute | solution.py:12
  163.3 6.5 %collective-permute-start.15 = (f32[1,34,64]{2,1,0:T(8,128)S(1)}, f32[1,34,64]{2,1,0:T(8,128)S(1)}, u32[]{:S(2)}, u32[]{:S(2)}) collective-permute-start(f32[1,34,64]{2,1,0:T(8,128)S(1)} %get-tuple-element.34), channel_id=1, source_target_pairs={{0,4},{4,8},{8,12},{12,16},{16,20},{20,24},{24,28},{1,5},{5,9},{9,... | collective-permute-start | bytes 26120 | tf_op jit(solution)/shard_map/ppermute | solution.py:20
  167.1 5.1 %collective-permute-start.16 = (f32[1,34,64]{2,1,0:T(8,128)S(1)}, f32[1,34,64]{2,1,0:T(8,128)S(1)}, u32[]{:S(2)}, u32[]{:S(2)}) collective-permute-start(f32[1,34,64]{2,1,0:T(8,128)S(1)} %get-tuple-element.35), channel_id=1, source_target_pairs={{4,0},{8,4},{12,8},{16,12},{20,16},{24,20},{28,24},{5,1},{9,5},{13... | collective-permute-start | bytes 26120 | tf_op jit(solution)/shard_map/ppermute | solution.py:23
  169.1 3.9 %collective-permute-start.17 = (f32[16,16,64]{2,1,0:T(8,128)S(1)}, f32[16,16,64]{2,1,0:T(8,128)S(1)}, u32[]{:S(2)}, u32[]{:S(2)}) collective-permute-start(f32[16,16,64]{2,1,0:T(8,128)S(1)} %broadcast_multiply_fusion.2), channel_id=1, source_target_pairs={{0,1},{1,0},{2,3},{3,2},{4,5},{5,4},{6,7},{7,6},{8,9},{9,8},{10,11... | collective-permute-start | bytes 196616 | tf_op jit(solution)/shard_map/ppermute | solution.py:35
  173.8 5.6 %collective-permute-start.18 = (f32[16,1,64]{2,1,0:T(1,128)S(1)}, f32[16,1,64]{2,1,0:T(1,128)S(1)}, u32[]{:S(2)}, u32[]{:S(2)}) collective-permute-start(f32[16,1,64]{2,1,0:T(1,128)S(1)} %get-tuple-element.36), channel_id=1, source_target_pairs={{0,2},{1,3},{4,6},{5,7},{8,10},{9,11},{12,14},{13,15},{16,18},{17,... | collective-permute-start | bytes 12296 | tf_op jit(solution)/shard_map/ppermute | solution.py:12
  178.0 4.4 %collective-permute-start.19 = (f32[16,1,64]{2,1,0:T(1,128)S(1)}, f32[16,1,64]{2,1,0:T(1,128)S(1)}, u32[]{:S(2)}, u32[]{:S(2)}) collective-permute-start(f32[16,1,64]{2,1,0:T(1,128)S(1)} %get-tuple-element.37), channel_id=1, source_target_pairs={{2,0},{3,1},{6,4},{7,5},{10,8},{11,9},{14,12},{15,13},{18,16},{19,... | collective-permute-start | bytes 12296 | tf_op jit(solution)/shard_map/ppermute | solution.py:12
  182.4 8.6 %collective-permute-start.20 = (f32[1,34,64]{2,1,0:T(8,128)S(1)}, f32[1,34,64]{2,1,0:T(8,128)S(1)}, u32[]{:S(2)}, u32[]{:S(2)}) collective-permute-start(f32[1,34,64]{2,1,0:T(8,128)S(1)} %get-tuple-element.30), channel_id=1, source_target_pairs={{0,4},{4,8},{8,12},{12,16},{16,20},{20,24},{24,28},{1,5},{5,9},{9,... | collective-permute-start | bytes 26120 | tf_op jit(solution)/shard_map/ppermute | solution.py:20
  189.1 5.1 %collective-permute-start.21 = (f32[1,34,64]{2,1,0:T(8,128)S(1)}, f32[1,34,64]{2,1,0:T(8,128)S(1)}, u32[]{:S(2)}, u32[]{:S(2)}) collective-permute-start(f32[1,34,64]{2,1,0:T(8,128)S(1)} %get-tuple-element.31), channel_id=1, source_target_pairs={{4,0},{8,4},{12,8},{16,12},{20,16},{24,20},{28,24},{5,1},{9,5},{13... | collective-permute-start | bytes 26120 | tf_op jit(solution)/shard_map/ppermute | solution.py:23
  209.3 14.2 %collective-permute-start.22 = (f32[8,16,32]{2,1,0:T(8,128)S(1)}, f32[8,16,32]{2,1,0:T(8,128)S(1)}, u32[]{:S(2)}, u32[]{:S(2)}) collective-permute-start(f32[8,16,32]{2,1,0:T(8,128)S(1)} %broadcast_multiply_fusion.5), channel_id=1, source_target_pairs={{0,2},{2,0},{1,3},{3,1},{4,6},{6,4},{5,7},{7,5},{8,10},{10,8},{9,1... | collective-permute-start | bytes 49160 | tf_op jit(solution)/shard_map/ppermute | solution.py:35
  223.7 5.9 %collective-permute-start.23 = (f32[1,34,32]{2,1,0:T(8,128)S(1)}, f32[1,34,32]{2,1,0:T(8,128)S(1)}, u32[]{:S(2)}, u32[]{:S(2)}) collective-permute-start(f32[1,34,32]{2,1,0:T(8,128)S(1)} %get-tuple-element.42), channel_id=1, source_target_pairs={{0,4},{4,8},{8,12},{12,16},{16,20},{20,24},{24,28},{1,5},{5,9},{9,... | collective-permute-start | bytes 13064 | tf_op jit(solution)/shard_map/ppermute | solution.py:20
  225.6 5.4 %collective-permute-start.24 = (f32[1,34,32]{2,1,0:T(8,128)S(1)}, f32[1,34,32]{2,1,0:T(8,128)S(1)}, u32[]{:S(2)}, u32[]{:S(2)}) collective-permute-start(f32[1,34,32]{2,1,0:T(8,128)S(1)} %get-tuple-element.43), channel_id=1, source_target_pairs={{4,0},{8,4},{12,8},{16,12},{20,16},{24,20},{28,24},{5,1},{9,5},{13... | collective-permute-start | bytes 13064 | tf_op jit(solution)/shard_map/ppermute | solution.py:23
  228.0 3.9 %collective-permute-start.25 = (f32[8,16,32]{2,1,0:T(8,128)S(1)}, f32[8,16,32]{2,1,0:T(8,128)S(1)}, u32[]{:S(2)}, u32[]{:S(2)}) collective-permute-start(f32[8,16,32]{2,1,0:T(8,128)S(1)} %broadcast_multiply_fusion.4), channel_id=1, source_target_pairs={{0,2},{2,0},{1,3},{3,1},{4,6},{6,4},{5,7},{7,5},{8,10},{10,8},{9,1... | collective-permute-start | bytes 49160 | tf_op jit(solution)/shard_map/ppermute | solution.py:35
  232.6 5.6 %collective-permute-start.26 = (f32[1,34,32]{2,1,0:T(8,128)S(1)}, f32[1,34,32]{2,1,0:T(8,128)S(1)}, u32[]{:S(2)}, u32[]{:S(2)}) collective-permute-start(f32[1,34,32]{2,1,0:T(8,128)S(1)} %get-tuple-element.40), channel_id=1, source_target_pairs={{0,4},{4,8},{8,12},{12,16},{16,20},{20,24},{24,28},{1,5},{5,9},{9,... | collective-permute-start | bytes 13064 | tf_op jit(solution)/shard_map/ppermute | solution.py:20
  236.3 5.1 %collective-permute-start.27 = (f32[1,34,32]{2,1,0:T(8,128)S(1)}, f32[1,34,32]{2,1,0:T(8,128)S(1)}, u32[]{:S(2)}, u32[]{:S(2)}) collective-permute-start(f32[1,34,32]{2,1,0:T(8,128)S(1)} %get-tuple-element.41), channel_id=1, source_target_pairs={{4,0},{8,4},{12,8},{16,12},{20,16},{24,20},{28,24},{5,1},{9,5},{13... | collective-permute-start | bytes 13064 | tf_op jit(solution)/shard_map/ppermute | solution.py:23
  243.6 5.7 %collective-permute-start.28 = (f32[1,18,16]{2,1,0:T(8,128)S(1)}, f32[1,18,16]{2,1,0:T(8,128)S(1)}, u32[]{:S(2)}, u32[]{:S(2)}) collective-permute-start(f32[1,18,16]{2,1,0:T(8,128)S(1)} %get-tuple-element.52), channel_id=1, source_target_pairs={{0,4},{4,8},{8,12},{12,16},{16,20},{20,24},{24,28},{1,5},{5,9},{9,... | collective-permute-start | bytes 3464 | tf_op jit(solution)/shard_map/ppermute | solution.py:20
  245.5 5.0 %collective-permute-start.29 = (f32[1,18,16]{2,1,0:T(8,128)S(1)}, f32[1,18,16]{2,1,0:T(8,128)S(1)}, u32[]{:S(2)}, u32[]{:S(2)}) collective-permute-start(f32[1,18,16]{2,1,0:T(8,128)S(1)} %get-tuple-element.53), channel_id=1, source_target_pairs={{4,0},{8,4},{12,8},{16,12},{20,16},{24,20},{28,24},{5,1},{9,5},{13... | collective-permute-start | bytes 3464 | tf_op jit(solution)/shard_map/ppermute | solution.py:23
  250.8 5.0 %collective-permute-start.30 = (f32[1,18,16]{2,1,0:T(8,128)S(1)}, f32[1,18,16]{2,1,0:T(8,128)S(1)}, u32[]{:S(2)}, u32[]{:S(2)}) collective-permute-start(f32[1,18,16]{2,1,0:T(8,128)S(1)} %get-tuple-element.50), channel_id=1, source_target_pairs={{0,4},{4,8},{8,12},{12,16},{16,20},{20,24},{24,28},{1,5},{5,9},{9,... | collective-permute-start | bytes 3464 | tf_op jit(solution)/shard_map/ppermute | solution.py:20
  252.8 5.0 %collective-permute-start.31 = (f32[1,18,16]{2,1,0:T(8,128)S(1)}, f32[1,18,16]{2,1,0:T(8,128)S(1)}, u32[]{:S(2)}, u32[]{:S(2)}) collective-permute-start(f32[1,18,16]{2,1,0:T(8,128)S(1)} %get-tuple-element.51), channel_id=1, source_target_pairs={{4,0},{8,4},{12,8},{16,12},{20,16},{24,20},{28,24},{5,1},{9,5},{13... | collective-permute-start | bytes 3464 | tf_op jit(solution)/shard_map/ppermute | solution.py:23
  258.4 5.2 %collective-permute-start.32 = (f32[1,10,8]{2,1,0:T(8,128)S(1)}, f32[1,10,8]{2,1,0:T(8,128)S(1)}, u32[]{:S(2)}, u32[]{:S(2)}) collective-permute-start(f32[1,10,8]{2,1,0:T(8,128)S(1)} %get-tuple-element.63), channel_id=1, source_target_pairs={{0,4},{4,8},{8,12},{12,16},{16,20},{20,24},{24,28},{1,5},{5,9},{9,... | collective-permute-start | bytes 968 | tf_op jit(solution)/shard_map/ppermute | solution.py:20
  260.3 5.0 %collective-permute-start.33 = (f32[1,10,8]{2,1,0:T(8,128)S(1)}, f32[1,10,8]{2,1,0:T(8,128)S(1)}, u32[]{:S(2)}, u32[]{:S(2)}) collective-permute-start(f32[1,10,8]{2,1,0:T(8,128)S(1)} %get-tuple-element.64), channel_id=1, source_target_pairs={{4,0},{8,4},{12,8},{16,12},{20,16},{24,20},{28,24},{5,1},{9,5},{13... | collective-permute-start | bytes 968 | tf_op jit(solution)/shard_map/ppermute | solution.py:23
  265.5 5.0 %collective-permute-start.34 = (f32[1,10,8]{2,1,0:T(8,128)S(1)}, f32[1,10,8]{2,1,0:T(8,128)S(1)}, u32[]{:S(2)}, u32[]{:S(2)}) collective-permute-start(f32[1,10,8]{2,1,0:T(8,128)S(1)} %get-tuple-element.61), channel_id=1, source_target_pairs={{0,4},{4,8},{8,12},{12,16},{16,20},{20,24},{24,28},{1,5},{5,9},{9,... | collective-permute-start | bytes 968 | tf_op jit(solution)/shard_map/ppermute | solution.py:20
  267.5 5.0 %collective-permute-start.35 = (f32[1,10,8]{2,1,0:T(8,128)S(1)}, f32[1,10,8]{2,1,0:T(8,128)S(1)}, u32[]{:S(2)}, u32[]{:S(2)}) collective-permute-start(f32[1,10,8]{2,1,0:T(8,128)S(1)} %get-tuple-element.62), channel_id=1, source_target_pairs={{4,0},{8,4},{12,8},{16,12},{20,16},{24,20},{28,24},{5,1},{9,5},{13... | collective-permute-start | bytes 968 | tf_op jit(solution)/shard_map/ppermute | solution.py:23
where the time goes:
time: 274 us; the launch traced here: 273 us
  local copies, waits for them, and re-layouts  96.3 us (35%)
  starting transfers between devices  85.2 us (31%)
  other arithmetic  47.3 us (17%)
  waiting for transfers between devices  42.8 us (16%)
    reshape x5, local copies, waits for them, and re-layouts, restrict(): values.reshape(size_a // 2, 2, size_b // 2, 2, size_c // 2, 2)  81.1 us
    ppermute x11, starting transfers between devices, extended(): lax.ppermute(lax.slice_in_dim(block, block.shape[dim] - width, None, axis...  35.7 us
    reduce_sum x8, other arithmetic, restrict(): values.reshape(size_a // 2, 2, size_b // 2, 2, size_c // 2, 2)  33.2 us
    ppermute x11, waiting for transfers between devices, extended(): lax.ppermute(lax.slice_in_dim(block, 0, width, axis=dim), axis, backward)  25.7 us
    ppermute x11, starting transfers between devices, extended(): lax.ppermute(lax.slice_in_dim(block, 0, width, axis=dim), axis, backward)  23.4 us
    ppermute x10, starting transfers between devices, passed_along(): return lax.ppermute(block, axis, route)  23.1 us
    ppermute x10, waiting for transfers between devices, passed_along(): return lax.ppermute(block, axis, route)  12.6 us
    select_n x2, local copies, waits for them, and re-layouts, merge_pairs(): jnp.where(upper_half, jnp.concatenate([theirs_reaction, coarse_reaction],...  11.2 us
  transfers between devices with their start and end apart: 36, of which 18 were waited for; matrix products, arithmetic and copies ran while one was open for 24% of the time, Pallas kernels for 0%

commit v1 on v0

v1 whole, which is shorter than its diff:
```python
import functools

import jax
import jax.numpy as jnp
from jax import lax
from jax.experimental import pallas as pl
from jax.experimental.pallas import tpu as pltpu
from jax.sharding import PartitionSpec as P

LEVELS = 4
MESH = pl.DeviceIdType.MESH
NEAR = [(dx, dy) for dx in (-1, 0, 1) for dy in (-1, 0, 1) if (dx, dy) != (0, 0)]
WIDE = [(dx, dy) for dx in range(-2, 3) for dy in range(-2, 3) if (dx, dy) != (0, 0)]


def coefficients(level_index):
    upper_edge = 1.1 * (2.0 + 0.02 * 4.0**level_index)
    lower_edge = upper_edge / 8.0
    midpoint = (upper_edge + lower_edge) / 2.0
    half_span = (upper_edge - lower_edge) / 2.0
    sigma_value = midpoint / half_span
    rho_first = 1.0 / sigma_value
    rho_second = 1.0 / (2.0 * sigma_value - rho_first)
    return (midpoint, rho_second * rho_first, 2.0 * rho_second / half_span)


def row_ids(shape):
    return lax.broadcasted_iota(jnp.int32, shape, len(shape) - 2)


def lane_ids(shape):
    return lax.broadcasted_iota(jnp.int32, shape, len(shape) - 1)


def roll(value, shift, dim):
    size = value.shape[dim]
    shift = shift % size
    return value if shift == 0 else pltpu.roll(value, shift, dim)


def slot_place(slot, width):
    if width == 1:
        return slot, 0
    return 2 * (slot % 4), slot // 4


def slot_mask(slot, width):
    row, half = slot_place(slot, width)
    rows, lanes = row_ids((8, 128)), lane_ids((8, 128))
    mask = (rows >= row) & (rows < row + width)
    if width > 1:
        mask = mask & ((lanes >= 64) if half else (lanes < 64))
    return mask


def unpacked(tile, slot, width, low):
    row, half = slot_place(slot, width)
    rows, lanes = row_ids((8, 128)), lane_ids((8, 128))
    value = roll(tile, (8 - width if low else 0) - row, 0)
    if half:
        value = roll(value, 64, 1)
    mask = (rows >= 8 - width) if low else (rows < width)
    if width > 1:
        mask = mask & (lanes < 64)
    return jnp.where(mask, value, 0.0)


class Halo:
    def __init__(self, place, block, width, packs, sides, corners, send, recv):
        self.place, self.block, self.width = place, block, width
        self.packs, self.sides, self.corners = packs, sides, corners
        self.send, self.recv = send, recv
        self.planes = block.shape[0] - 2 * width
        self.rows = block.shape[1] - 16

    def clear(self):
        w, planes = self.width, self.planes
        edge = jnp.zeros((w,) + self.block.shape[1:], jnp.float32)
        self.block[0:w] = edge
        self.block[planes + w : planes + 2 * w] = edge
        self.sides[...] = jnp.zeros(self.sides.shape, jnp.float32)
        self.corners[...] = jnp.zeros(self.corners.shape, jnp.float32)

    def copy(self, number):
        dx, dy = NEAR[number]
        w, planes, rows, block = self.width, self.planes, self.rows, self.block
        if dy == 0:
            source = block.at[planes : planes + w] if dx > 0 else block.at[w : 2 * w]
            target = block.at[0:w] if dx > 0 else block.at[planes + w : planes + 2 * w]
            source, target = source.at[:, 8 : 8 + rows], target.at[:, 8 : 8 + rows]
        else:
            pack = self.packs.at[0 if dy > 0 else 1]
            if dx == 0:
                source, target = pack, self.sides.at[0 if dy > 0 else 1]
            else:
                source = pack.at[planes // 8 - 1 if dx > 0 else 0]
                target = self.corners.at[(0 if dx > 0 else 2) + (0 if dy > 0 else 1)]
        return pltpu.make_async_remote_copy(
            src_ref=source,
            dst_ref=target,
            send_sem=self.send.at[number],
            recv_sem=self.recv.at[number],
            device_id=self.place.device(dx, dy),
            device_id_type=MESH,
        )

    def start(self):
        w, rows = self.width, self.rows
        for number, (dx, dy) in enumerate(NEAR):
            if dy == 0:
                pl.when(self.place.has(dx, dy))(lambda n=number: self.copy(n).start())
        for tile in range(self.planes // 8):
            high = jnp.zeros((8, 128), jnp.float32)
            low = high
            for slot in range(8):
                row, half = slot_place(slot, w)
                mask = slot_mask(slot, w)
                plane = w + 8 * tile + slot
                last = roll(self.block[plane, rows : rows + 8, :], row + w - 8, 0)
                first = roll(self.block[plane, 8:16, :], row, 0)
                if half:
                    last, first = roll(last, 64, 1), roll(first, 64, 1)
                high = jnp.where(mask, last, high)
                low = jnp.where(mask, first, low)
            self.packs[0, tile] = high
            self.packs[1, tile] = low
        for number, (dx, dy) in enumerate(NEAR):
            if dy != 0:
                pl.when(self.place.has(dx, dy))(lambda n=number: self.copy(n).start())

    def finish(self):
        w, planes, rows = self.width, self.planes, self.rows
        for number, (dx, dy) in enumerate(NEAR):
            pl.when(self.place.has(-dx, -dy))(lambda n=number: self.copy(n).wait_recv())
        for tile in range(planes // 8):
            low, high = self.sides[0, tile], self.sides[1, tile]
            for slot in range(8):
                plane = w + 8 * tile + slot
                self.block[plane, 0:8, :] = unpacked(low, slot, w, True)
                self.block[plane, rows + 8 : rows + 16, :] = unpacked(high, slot, w, False)
        for side in (0, 1):
            low, high = self.corners[2 * side], self.corners[2 * side + 1]
            for index in range(w):
                slot = 8 - w + index if side == 0 else index
                plane = index if side == 0 else planes + w + index
                self.block[plane, 0:8, :] = unpacked(low, slot, w, True)
                self.block[plane, rows + 8 : rows + 16, :] = unpacked(high, slot, w, False)

    def drain(self):
        for number, (dx, dy) in enumerate(NEAR):
            pl.when(self.place.has(dx, dy))(lambda n=number: self.copy(n).wait_send())


class Gather:
    def __init__(self, place, tiles, send, recv):
        self.place, self.tiles, self.send, self.recv = place, tiles, send, recv

    def clear(self):
        self.tiles[...] = jnp.zeros(self.tiles.shape, jnp.float32)

    def copy(self, number):
        dx, dy = WIDE[number]
        return pltpu.make_async_remote_copy(
            src_ref=self.tiles.at[2, 2],
            dst_ref=self.tiles.at[2 - dx, 2 - dy],
            send_sem=self.send.at[number],
            recv_sem=self.recv.at[number],
            device_id=self.place.device(dx, dy),
            device_id_type=MESH,
        )

    def start(self, tile):
        self.tiles[2, 2] = tile
        for number, (dx, dy) in enumerate(WIDE):
            pl.when(self.place.has(dx, dy))(lambda n=number: self.copy(n).start())

    def finish(self, field):
        for number, (dx, dy) in enumerate(WIDE):
            pl.when(self.place.has(-dx, -dy))(lambda n=number: self.copy(n).wait_recv())
        field[...] = jnp.zeros(field.shape, jnp.float32)
        rows, lanes = row_ids((8, 128)), lane_ids((8, 128))
        for bx in range(5):
            for group in range(3):
                pair = [self.tiles[bx, by] for by in range(2 * group, min(2 * group + 2, 5))]
                for index in range(4):
                    total = jnp.zeros((8, 128), jnp.float32)
                    for where, tile in enumerate(pair):
                        value = roll(tile, 4 * where - 4 * (index % 2), 0)
                        if index >= 2:
                            value = roll(value, 64, 1)
                        mask = (rows >= 4 * where) & (rows < 4 * where + 4) & (lanes < 64)
                        total = jnp.where(mask, value, total)
                    field[4 * bx + index, 8 * group : 8 * group + 8, :] = total

    def drain(self):
        for number, (dx, dy) in enumerate(WIDE):
            pl.when(self.place.has(dx, dy))(lambda n=number: self.copy(n).wait_send())


class Place:
    def __init__(self, counts):
        self.counts = counts
        self.box, self.agg = lax.axis_index("box"), lax.axis_index("agg")

    def device(self, dx, dy):
        return (self.box + dx, self.agg + dy)

    def has(self, dx, dy):
        x, y = self.device(dx, dy)
        return (x >= 0) & (x < self.counts[0]) & (y >= 0) & (y < self.counts[1])

    def barrier(self):
        semaphore = pltpu.get_barrier_semaphore()
        for dx, dy in WIDE:

            @pl.when(self.has(dx, dy))
            def _(dx=dx, dy=dy):
                pl.semaphore_signal(
                    semaphore, inc=1, device_id=self.device(dx, dy), device_id_type=MESH
                )

        spans = []
        for at, count in zip((self.box, self.agg), self.counts):
            spans.append(1 + jnp.minimum(at, 2) + jnp.minimum(count - 1 - at, 2))
        pl.semaphore_wait(semaphore, spans[0] * spans[1] - 1)


def weighted(block, plane, wrap):
    middle = block[plane]
    total = (block[plane - 1] + block[plane + 1]) + (middle + middle)
    total = (roll(total, 1, 0) + roll(total, -1, 0)) + (total + total)
    if wrap:
        total = total[8:-8]
        lanes = lane_ids(total.shape)
        left = jnp.where(lanes == 0, 0.0, roll(total, 1, 1))
        right = jnp.where(lanes == 127, 0.0, roll(total, -1, 1))
    else:
        left, right = roll(total, 1, 1), roll(total, -1, 1)
    return (left + right) + (total + total), middle


def paired(flat, extent):
    half = flat.shape[0] // 2
    rows = flat[pl.ds(0, half, stride=2), :] + flat[pl.ds(1, half, stride=2), :]
    source, target = row_ids((128, 128)), lane_ids((128, 128))
    pairs = (source < extent) & ((source == 2 * target) | (source == 2 * target + 1))
    return jnp.dot(
        rows,
        jnp.where(pairs, 0.5, 0.0),
        precision=lax.Precision.HIGHEST,
        preferred_element_type=jnp.float32,
    )


def in_grid(start, stop, shape, extent):
    rows, lanes = row_ids(shape), lane_ids(shape)
    return jnp.where((rows >= start) & (rows < stop) & (lanes < extent), 1.0, 0.0)


def plane_in_grid(index, count):
    return jnp.where((index >= 0) & (index < count), 1.0, 0.0)


def each(start, stop, body, step=2):
    whole = (stop - start) // step

    def several(index, _):
        for offset in range(step):
            body(start + index * step + offset)
        return 0

    lax.fori_loop(0, whole, several, 0)
    for index in range(start + whole * step, stop):
        body(index)


def kernel(
    counts,
    flags, source, guess, reaction,
    iterate, out_one, out_two, out_three, out_four, out_bottom,
    field_a, field_b, field_c, step_one,
    f_one, k_one, e_one, f_two, k_two, e_two,
    f_three, k_three, e_three, f_four, k_four, e_four,
    flat_zero, flat_one, flat_two, flat_three, flat_extra,
    packs_zero, sides_zero, packs_one, sides_one, packs_two, sides_two, corners,
    tiles, near_send, near_recv, wide_send, wide_recv,
):
    place = Place(counts)
    planes, rows, depth = source.shape

    def halo(number, block, width, packs, sides, index):
        return Halo(
            place, block, width, packs.at[index], sides.at[index], corners.at[number],
            near_send.at[number], near_recv.at[number],
        )

    halo_a = halo(0, field_a, 1, packs_zero, sides_zero, 0)
    halo_b = halo(1, field_b, 1, packs_zero, sides_zero, 1)
    halo_c = halo(2, field_c, 1, packs_zero, sides_zero, 2)
    halo_f_one = halo(3, f_one, 2, packs_one, sides_one, 0)
    halo_k_one = halo(4, k_one, 2, packs_one, sides_one, 1)
    halo_f_two = halo(5, f_two, 2, packs_two, sides_two, 0)
    halo_k_two = halo(6, k_two, 2, packs_two, sides_two, 1)
    gather_f = Gather(place, tiles.at[0], wide_send.at[0], wide_recv.at[0])
    gather_k = Gather(place, tiles.at[1], wide_send.at[1], wide_recv.at[1])
    exchanges = [
        halo_a, halo_b, halo_c, halo_f_one, halo_k_one, halo_f_two, halo_k_two, gather_f, gather_k,
    ]
    for exchange in exchanges:
        exchange.clear()

    lanes = lane_ids((rows, depth))
    patch = depth // flags.shape[2]
    refined = jnp.zeros((rows, depth), jnp.float32)
    for box in range(flags.shape[2]):
        chosen = (lanes >= box * patch) & (lanes < (box + 1) * patch)
        refined = refined + jnp.where(chosen, flags[0, 0, box].astype(jnp.float32), 0.0)

    def stage(plane):
        field_a[plane + 1, 8 : 8 + rows, :] = guess[plane]

    each(0, planes, stage, 4)
    place.barrier()
    halo_a.start()

    def spread(flat, target, count, extent):
        values = paired(flat, extent)
        target[2 : 2 + count, 8 : 8 + count, :] = values.reshape(count, count, 128)

    def coarse_reaction(plane):
        flat_zero[pl.ds(pl.multiple_of(plane * rows, rows), rows), :] = (
            reaction[2 * plane] + reaction[2 * plane + 1]
        )

    one, two, three = planes // 2, planes // 4, planes // 8
    each(0, one, coarse_reaction)
    spread(flat_zero, k_one, one, depth)
    halo_k_one.start()
    for plane in range(two):
        flat_one[plane * one : (plane + 1) * one, :] = (
            k_one[2 + 2 * plane, 8 : 8 + one, :] + k_one[3 + 2 * plane, 8 : 8 + one, :]
        )
    spread(flat_one, k_two, two, depth // 2)
    halo_k_two.start()
    for plane in range(three):
        flat_two[plane * two : (plane + 1) * two, :] = (
            k_two[2 + 2 * plane, 8 : 8 + two, :] + k_two[3 + 2 * plane, 8 : 8 + two, :]
        )
    small = paired(flat_two, depth // 4)
    gather_k.start(small[0:8] + roll(small[8:16], 64, 1))

    midpoint, factor_one, factor_two = coefficients(0)

    def fine_residual(block, plane):
        total, middle = weighted(block, plane + 1, True)
        middle = middle[8:-8]
        applied = (8.0 / 7.0 + reaction[plane]) * middle - total * (1.0 / 56.0)
        return refined * (source[plane] - applied), middle

    halo_a.finish()

    def first(plane):
        residual, middle = fine_residual(field_a, plane)
        step = residual * (1.0 / midpoint)
        step_one[plane] = step
        field_b[plane + 1, 8 : 8 + rows, :] = middle + step

    each(0, planes, first)
    halo_b.start()
    halo_b.finish()

    def second(plane):
        residual, middle = fine_residual(field_b, plane)
        value = middle + (factor_one * step_one[plane] + factor_two * residual)
        field_c[plane + 1, 8 : 8 + rows, :] = value
        iterate[plane] = value

    each(0, planes, second)
    halo_c.start()
    halo_c.finish()

    def third(plane):
        total = fine_residual(field_c, 2 * plane)[0] + fine_residual(field_c, 2 * plane + 1)[0]
        flat_zero[pl.ds(pl.multiple_of(plane * rows, rows), rows), :] = total

    each(0, one, third, 1)
    spread(flat_zero, f_one, one, depth)
    halo_f_one.start()

    def correct(level, f, k, e, plane, mask):
        midpoint, factor_one, factor_two = coefficients(level)
        slope = factor_two / midpoint
        keep = (1.0 + factor_one) / midpoint + factor_two - slope * 8.0 / 7.0
        total, middle = weighted(f, plane, False)
        value = (keep - slope * k[plane]) * middle + (slope / 56.0) * total
        e[plane] = value * mask

    def left_over(f, k, e, plane):
        total, middle = weighted(e, plane, False)
        return f[plane] - ((8.0 / 7.0 + k[plane]) * middle - total * (1.0 / 56.0))

    halo_k_one.finish()
    halo_k_two.finish()
    gather_k.finish(k_three)
    for level, f, k, e, exchange, out, flat, size in (
        (1, f_one, k_one, e_one, halo_f_one, out_one, flat_one, one),
        (2, f_two, k_two, e_two, halo_f_two, out_two, flat_two, two),
    ):
        extent = depth >> level
        exchange.finish()
        row_mask = in_grid(
            8 - place.agg * size, 8 + (counts[1] - place.agg) * size, f.shape[1:], extent
        )

        def one_plane(plane, level=level, f=f, k=k, e=e, size=size, row_mask=row_mask):
            at = plane_in_grid(place.box * size + plane - 2, counts[0] * size)
            correct(level, f, k, e, plane, row_mask * at)

        each(1, size + 3, one_plane)
        out[...] = e[2 : 2 + size, 8 : 8 + size, 0:extent]

        def remainder(plane, f=f, k=k, e=e, size=size, flat=flat):
            total = left_over(f, k, e, 2 * plane + 2) + left_over(f, k, e, 2 * plane + 3)
            flat[pl.ds(pl.multiple_of(plane * size, size), size), :] = total[8 : 8 + size]

        each(0, size // 2, remainder, 1)
        if level == 1:
            spread(flat, f_two, size // 2, extent)
            halo_f_two.start()
        else:
            small = paired(flat, extent)
            gather_f.start(small[0:8] + roll(small[8:16], 64, 1))

    gather_f.finish(f_three)
    mask_three = in_grid(
        8 - place.agg * three, 8 + (counts[1] - place.agg) * three, f_three.shape[1:], depth // 8
    )

    def at_three(plane):
        return mask_three * plane_in_grid(place.box * three + plane - 8, counts[0] * three)

    for plane in range(3, 17):
        correct(3, f_three, k_three, e_three, plane, at_three(plane))
    out_three[...] = e_three[8:12, 8:12, 0 : depth // 8]
    flat_three[...] = jnp.zeros(flat_three.shape, jnp.float32)
    flat_extra[...] = jnp.zeros(flat_extra.shape, jnp.float32)
    for plane in range(6):
        total = jnp.zeros(f_three.shape[1:], jnp.float32)
        for child in (4 + 2 * plane, 5 + 2 * plane):
            total = total + left_over(f_three, k_three, e_three, child) * at_three(child)
        flat_three[32 * plane : 32 * plane + 24, :] = total
        flat_extra[32 * plane : 32 * plane + 24, :] = (
            k_three[4 + 2 * plane] + k_three[5 + 2 * plane]
        )
    f_four[...] = paired(flat_three, depth // 8).reshape(6, 16, 128)
    k_four[...] = paired(flat_extra, depth // 8).reshape(6, 16, 128)

    four = three // 2
    mask_four = in_grid(
        4 - place.agg * four, 4 + (counts[1] - place.agg) * four, f_four.shape[1:], depth // 16
    )
    for plane in range(1, 5):
        at = plane_in_grid(place.box * four + plane - 2, counts[0] * four)
        correct(4, f_four, k_four, e_four, plane, mask_four * at)
    out_four[...] = e_four[2:4, 4:6, 0 : depth // 16]
    for plane in (2, 3):
        out_bottom[plane - 2] = left_over(f_four, k_four, e_four, plane)[4:6, 0 : depth // 16]
    for exchange in exchanges:
        exchange.drain()


def per_device(counts, source, guess, reaction, flags):
    planes, rows, depth = source.shape
    assert planes == rows and planes == 32 and depth == 128 and flags.shape[:2] == (1, 1)
    f32 = jnp.float32

    def vmem(*shape):
        return pltpu.VMEM(shape, f32)

    one, two = planes // 2, planes // 4
    scratch = [vmem(planes + 2, rows + 16, depth)] * 3 + [vmem(planes, rows, depth)]
    scratch += [vmem(one + 4, one + 16, 128)] * 3 + [vmem(two + 4, two + 16, 128)] * 3
    scratch += [vmem(20, 24, 128)] * 3 + [vmem(6, 16, 128)] * 3
    scratch += [vmem(one * rows, 128), vmem(two * one, 128), vmem(two // 2 * two, 128)]
    scratch += [vmem(192, 128)] * 2
    scratch += [vmem(3, 2, planes // 8, 8, 128)] * 2
    scratch += [vmem(2, 2, one // 8, 8, 128)] * 2 + [vmem(2, 2, two // 8, 8, 128)] * 2
    scratch += [vmem(7, 4, 8, 128), vmem(2, 5, 5, 8, 128)]
    scratch += [pltpu.SemaphoreType.DMA((7, 8))] * 2 + [pltpu.SemaphoreType.DMA((2, 24))] * 2
    outs = [jax.ShapeDtypeStruct(source.shape, f32)]
    for level in range(1, LEVELS + 1):
        outs.append(
            jax.ShapeDtypeStruct((planes >> level, rows >> level, depth >> level), f32)
        )
    outs.append(outs[-1])
    whole = pl.BlockSpec(memory_space=pltpu.VMEM)
    return tuple(
        pl.pallas_call(
            functools.partial(kernel, counts),
            out_shape=outs,
            in_specs=[pl.BlockSpec(memory_space=pltpu.SMEM)] + [whole] * 3,
            out_specs=[whole] * 6,
            scratch_shapes=scratch,
            compiler_params=pltpu.CompilerParams(
                collective_id=0, has_side_effects=True, vmem_limit_bytes=32 * 1024 * 1024
            ),
        )(flags, source, guess, reaction)
    )


def solution(mesh):
    spec = P("box", "agg", None)
    counts = (mesh.shape["box"], mesh.shape["agg"])
    return jax.shard_map(
        functools.partial(per_device, counts),
        mesh=mesh,
        in_specs=(spec,) * 4,
        out_specs=(spec,) * 6,
        check_vma=False,
    )
```

time: 274 us -> 46.3 us (0.17)
  local copies, waits for them, and re-layouts: 96.3 us -> 7.59 us
  starting transfers between devices: 85.2 us -> 0 us
  other arithmetic: 47.3 us -> 0 us
  waiting for transfers between devices: 42.8 us -> 0 us
  Pallas kernels: 0 us -> 37.5 us
    ppermute x36 -> x0, starting transfers between devices: 85.2 us -> none  [the longest x11 35.7 us: extended(): lax.ppermute(lax.slice_in_dim(block, block.shape[dim] - width, None, axis...]
    reshape x5 -> x0, local copies, waits for them, and re-layouts: 81.1 us -> none  [restrict(): values.reshape(size_a // 2, 2, size_b // 2, 2, size_c // 2, 2)]
    ppermute x36 -> x0, waiting for transfers between devices: 42.8 us -> none  [the longest x11 25.7 us: extended(): lax.ppermute(lax.slice_in_dim(block, 0, width, axis=dim), axis, backward)]
    pallas_call x0 -> x1, Pallas kernels: none -> 37.5 us  [per_device(): pl.pallas_call(functools.partial(kernel, counts), out_shape=outs, in_spec...]
    reduce_sum x8 -> x0, other arithmetic: 33.2 us -> none  [restrict(): values.reshape(size_a // 2, 2, size_b // 2, 2, size_c // 2, 2)]
    select_n x2 -> x0, local copies, waits for them, and re-layouts: 11.2 us -> none  [merge_pairs(): jnp.where(upper_half, jnp.concatenate([theirs_reaction, coarse_reaction],...]
    unnamed x8 -> x14, local copies, waits for them, and re-layouts: 0.63 us -> 7.59 us
    add x4 -> x0, other arithmetic: 4.25 us -> none  [the longest x2 1.45 us: per_device(): correction = first_step + second_step]
  transfers between devices with their start and end apart: 36 -> 0, of which waited for: 18 -> 0; matrix products, arithmetic and copies ran while one was open for 24% -> 0% of each run, Pallas kernels for 0% -> 0%
where the time goes in v1:
time: 46.3 us; the launch traced here: 45.7 us
  Pallas kernels  37.5 us (81%)
  local copies, waits for them, and re-layouts  7.59 us (16%)
  between operations  0.65 us (1%)
    pallas_call x1, Pallas kernels, per_device(): pl.pallas_call(functools.partial(kernel, counts), out_shape=outs, in_spec...  37.5 us
    unnamed x14, local copies, waits for them, and re-layouts  7.59 us

profile of v1, /device:TPU:1, one launch (start us, length us, event | category | flops | bytes accessed | tf_op | source)
XLA Modules:
  0.0 45.7 jit_solution(13694440822764568472)
XLA Ops:
  0.6 0.0 copy-start
  0.6 1.0 %copy-done = f32[32,32,128]{2,1,0:T(8,128)S(1)} copy-done((f32[32,32,128]{2,1,0:T(8,128)S(1)}, f32[32,32,128]{2,1,0:T(8,128)}, u32[]{:S(2)}) %copy-start) | copy-done | bytes 524312
  1.7 0.0 copy-start.1
  1.7 1.0 %copy-done.1 = f32[32,32,128]{2,1,0:T(8,128)S(1)} copy-done((f32[32,32,128]{2,1,0:T(8,128)S(1)}, f32[32,32,128]{2,1,0:T(8,128)}, u32[]{:S(2)}) %copy-start.1) | copy-done | bytes 524312
  2.7 0.0 copy-start.2
  2.7 1.0 %copy-done.2 = f32[32,32,128]{2,1,0:T(8,128)S(1)} copy-done((f32[32,32,128]{2,1,0:T(8,128)S(1)}, f32[32,32,128]{2,1,0:T(8,128)}, u32[]{:S(2)}) %copy-start.2) | copy-done | bytes 524312
  3.8 0.0 copy-start.3
  3.8 0.7 %copy-done.3 = s32[1,1,4]{2,1,0:T(1,128)S(1)} copy-done((s32[1,1,4]{2,1,0:T(1,128)S(1)}, s32[1,1,4]{2,1,0:T(1,128)}, u32[]{:S(2)}) %copy-start.3) | copy-done | bytes 40
  4.4 37.5 %shard_map.91 = (f32[32,32,128]{2,1,0:T(8,128)S(1)}, f32[16,16,64]{2,1,0:T(8,128)S(1)}, f32[8,8,32]{2,1,0:T(8,128)S(1)}, f32[4,4,16]{2,1,0:T(4,128)S(1)}, f32[2,...) custom-call(s32[1,1,4]{2,1,0:T(1,128)S(1)} %copy-done.3, f32[32,32,128]{2,1,0:T(8,128)S(1)} %copy-done, ...), custom_call_target="tpu_custom_call" | custom-call | tf_op jit(solution)/shard_map/pallas_call | solution.py:498
  41.9 0.8 %copy.16 = f32[32,32,128]{2,1,0:T(8,128)} copy(f32[32,32,128]{2,1,0:T(8,128)S(1)} %get-tuple-element.12) | data formatting | bytes 1048576
  42.7 0.7 %copy.17 = f32[16,16,64]{2,1,0:T(8,128)} copy(f32[16,16,64]{2,1,0:T(8,128)S(1)} %get-tuple-element.13) | data formatting | bytes 131072
  43.3 0.6 %copy.18 = f32[8,8,32]{2,1,0:T(8,128)} copy(f32[8,8,32]{2,1,0:T(8,128)S(1)} %get-tuple-element.14) | data formatting | bytes 16384
  43.9 0.6 %copy.19 = f32[4,4,16]{2,1,0:T(4,128)} copy(f32[4,4,16]{2,1,0:T(4,128)S(1)} %get-tuple-element.15) | data formatting | bytes 2048
  44.5 0.6 %copy.20 = f32[2,2,8]{2,1,0:T(2,128)} copy(f32[2,2,8]{2,1,0:T(2,128)S(1)} %get-tuple-element.16) | data formatting | bytes 256
  45.1 0.6 %copy.21 = f32[2,2,8]{2,1,0:T(2,128)} copy(f32[2,2,8]{2,1,0:T(2,128)S(1)} %get-tuple-element.17) | data formatting | bytes 256
Async XLA Ops:
  0.6 1.0 %copy-start = (f32[32,32,128]{2,1,0:T(8,128)S(1)}, f32[32,32,128]{2,1,0:T(8,128)}, u32[]{:S(2)}) copy-start(f32[32,32,128]{2,1,0:T(8,128)} %source.1) | copy-start | bytes 1572868
  1.7 1.0 %copy-start.1 = (f32[32,32,128]{2,1,0:T(8,128)S(1)}, f32[32,32,128]{2,1,0:T(8,128)}, u32[]{:S(2)}) copy-start(f32[32,32,128]{2,1,0:T(8,128)} %guess.1) | copy-start | bytes 1572868
  2.7 1.0 %copy-start.2 = (f32[32,32,128]{2,1,0:T(8,128)S(1)}, f32[32,32,128]{2,1,0:T(8,128)}, u32[]{:S(2)}) copy-start(f32[32,32,128]{2,1,0:T(8,128)} %reaction.1) | copy-start | bytes 1572868
  3.8 0.7 %copy-start.3 = (s32[1,1,4]{2,1,0:T(1,128)S(1)}, s32[1,1,4]{2,1,0:T(1,128)}, u32[]{:S(2)}) copy-start(s32[1,1,4]{2,1,0:T(1,128)} %flags.1) | copy-start | bytes 52

commit v2 on v1

--- a/solution.py
+++ b/solution.py
@@ -225,29 +225,35 @@
         pl.semaphore_wait(semaphore, spans[0] * spans[1] - 1)
 
 
-def weighted(block, plane, wrap):
-    middle = block[plane]
-    total = (block[plane - 1] + block[plane + 1]) + (middle + middle)
-    total = (roll(total, 1, 0) + roll(total, -1, 0)) + (total + total)
-    if wrap:
-        total = total[8:-8]
-        lanes = lane_ids(total.shape)
-        left = jnp.where(lanes == 0, 0.0, roll(total, 1, 1))
-        right = jnp.where(lanes == 127, 0.0, roll(total, -1, 1))
-    else:
-        left, right = roll(total, 1, 1), roll(total, -1, 1)
-    return (left + right) + (total + total), middle
+def weighted(block, start, count, wrap):
+    held = [block[start - 1 + index] for index in range(count + 2)]
+    pairs = [low + high for low, high in zip(held[:-1], held[1:])]
+    results = []
+    for index in range(count):
+        total = pairs[index] + pairs[index + 1]
+        total = (roll(total, 1, 0) + roll(total, -1, 0)) + (total + total)
+        middle = held[index + 1]
+        if wrap:
+            total, middle = total[8:-8], middle[8:-8]
+            lanes = lane_ids(total.shape)
+            left = jnp.where(lanes == 0, 0.0, roll(total, 1, 1))
+            right = jnp.where(lanes == 127, 0.0, roll(total, -1, 1))
+        else:
+            left, right = roll(total, 1, 1), roll(total, -1, 1)
+        results.append(((left + right) + (total + total), middle))
+    return results
 
 
 def paired(flat, extent):
     half = flat.shape[0] // 2
     rows = flat[pl.ds(0, half, stride=2), :] + flat[pl.ds(1, half, stride=2), :]
-    source, target = row_ids((128, 128)), lane_ids((128, 128))
+    high = rows.astype(jnp.bfloat16)
+    low = (rows - high.astype(jnp.float32)).astype(jnp.bfloat16)
+    source, target = row_ids((256, 128)) % 128, lane_ids((256, 128))
     pairs = (source < extent) & ((source == 2 * target) | (source == 2 * target + 1))
     return jnp.dot(
-        rows,
-        jnp.where(pairs, 0.5, 0.0),
-        precision=lax.Precision.HIGHEST,
+        jnp.concatenate([high, low], axis=1),
+        jnp.where(pairs, 0.5, 0.0).astype(jnp.bfloat16),
         preferred_element_type=jnp.float32,
     )
 
@@ -261,29 +267,31 @@
     return jnp.where((index >= 0) & (index < count), 1.0, 0.0)
 
 
-def each(start, stop, body, step=2):
-    whole = (stop - start) // step
-
-    def several(index, _):
-        for offset in range(step):
-            body(start + index * step + offset)
+def groups(start, count, size, body):
+    assert count % size == 0
+    if count == size:
+        body(start)
+        return
+
+    def step(index, _):
+        body(start + index * size)
         return 0
 
-    lax.fori_loop(0, whole, several, 0)
-    for index in range(start + whole * step, stop):
-        body(index)
+    lax.fori_loop(0, count // size, step, 0)
 
 
 def kernel(
     counts,
-    flags, source, guess, reaction,
+    flags_in, source_in, guess_in, reaction_in,
     iterate, out_one, out_two, out_three, out_four, out_bottom,
+    flags, source, reaction,
     field_a, field_b, field_c, step_one,
     f_one, k_one, e_one, f_two, k_two, e_two,
     f_three, k_three, e_three, f_four, k_four, e_four,
     flat_zero, flat_one, flat_two, flat_three, flat_extra,
     packs_zero, sides_zero, packs_one, sides_one, packs_two, sides_two, corners,
-    tiles, near_send, near_recv, wide_send, wide_recv,
+    tiles, held_one, held_two, held_three, held_four, held_bottom,
+    near_send, near_recv, wide_send, wide_recv, local,
 ):
     place = Place(counts)
     planes, rows, depth = source.shape
@@ -303,108 +311,151 @@
     halo_k_two = halo(6, k_two, 2, packs_two, sides_two, 1)
     gather_f = Gather(place, tiles.at[0], wide_send.at[0], wide_recv.at[0])
     gather_k = Gather(place, tiles.at[1], wide_send.at[1], wide_recv.at[1])
-    exchanges = [
+    own_a = field_a.at[1 : 1 + planes, 8 : 8 + rows]
+    own_c = field_c.at[1 : 1 + planes, 8 : 8 + rows]
+    loads = [
+        pltpu.make_async_copy(origin, target, local.at[index])
+        for index, (origin, target) in enumerate(
+            ((guess_in, own_a), (reaction_in, reaction), (source_in, source), (flags_in, flags))
+        )
+    ]
+    stores = [
+        pltpu.make_async_copy(origin, target, local.at[4 + index])
+        for index, (origin, target) in enumerate(
+            (
+                (own_c, iterate), (held_one, out_one), (held_two, out_two),
+                (held_three, out_three), (held_four, out_four), (held_bottom, out_bottom),
+            )
+        )
+    ]
+    for load in loads:
+        load.start()
+    for exchange in (
         halo_a, halo_b, halo_c, halo_f_one, halo_k_one, halo_f_two, halo_k_two, gather_f, gather_k,
-    ]
-    for exchange in exchanges:
+    ):
         exchange.clear()
-
-    lanes = lane_ids((rows, depth))
-    patch = depth // flags.shape[2]
-    refined = jnp.zeros((rows, depth), jnp.float32)
-    for box in range(flags.shape[2]):
-        chosen = (lanes >= box * patch) & (lanes < (box + 1) * patch)
-        refined = refined + jnp.where(chosen, flags[0, 0, box].astype(jnp.float32), 0.0)
-
-    def stage(plane):
-        field_a[plane + 1, 8 : 8 + rows, :] = guess[plane]
-
-    each(0, planes, stage, 4)
+    flat_three[...] = jnp.zeros(flat_three.shape, jnp.float32)
+    flat_extra[...] = jnp.zeros(flat_extra.shape, jnp.float32)
     place.barrier()
+    loads[0].wait()
     halo_a.start()
 
     def spread(flat, target, count, extent):
         values = paired(flat, extent)
         target[2 : 2 + count, 8 : 8 + count, :] = values.reshape(count, count, 128)
 
-    def coarse_reaction(plane):
-        flat_zero[pl.ds(pl.multiple_of(plane * rows, rows), rows), :] = (
-            reaction[2 * plane] + reaction[2 * plane + 1]
-        )
+    def put(flat, plane, size, value):
+        flat[pl.ds(pl.multiple_of(plane * size, size), size), :] = value
 
     one, two, three = planes // 2, planes // 4, planes // 8
-    each(0, one, coarse_reaction)
+    loads[1].wait()
+
+    def coarse_reaction(start):
+        for plane in range(4):
+            at = start + plane
+            put(flat_zero, at, rows, reaction[2 * at] + reaction[2 * at + 1])
+
+    groups(0, one, 4, coarse_reaction)
     spread(flat_zero, k_one, one, depth)
     halo_k_one.start()
+    loads[2].wait()
+    loads[3].wait()
+
+    lanes = lane_ids((1, depth))
+    patch = depth // flags.shape[2]
+    refined = jnp.zeros((1, depth), jnp.float32)
+    for box in range(flags.shape[2]):
+        chosen = (lanes >= box * patch) & (lanes < (box + 1) * patch)
+        flag = flags[0, :, box : box + 1].astype(jnp.float32)
+        refined = refined + jnp.where(chosen, flag, 0.0)
+
+    midpoint, factor_one, factor_two = coefficients(0)
+
+    def fine_residuals(block, start, count):
+        results = []
+        for index, (total, middle) in enumerate(weighted(block, start + 1, count, True)):
+            applied = (8.0 / 7.0 + reaction[start + index]) * middle - total * (1.0 / 56.0)
+            results.append((refined * (source[start + index] - applied), middle))
+        return results
+
+    halo_a.finish()
+
+    def first(start):
+        for index, (residual, middle) in enumerate(fine_residuals(field_a, start, 8)):
+            step = residual * (1.0 / midpoint)
+            step_one[start + index] = step
+            field_b[start + index + 1, 8 : 8 + rows, :] = middle + step
+
+    groups(0, planes, 8, first)
+    halo_b.start()
+
     for plane in range(two):
-        flat_one[plane * one : (plane + 1) * one, :] = (
-            k_one[2 + 2 * plane, 8 : 8 + one, :] + k_one[3 + 2 * plane, 8 : 8 + one, :]
+        put(
+            flat_one, plane, one,
+            k_one[2 + 2 * plane, 8 : 8 + one, :] + k_one[3 + 2 * plane, 8 : 8 + one, :],
         )
     spread(flat_one, k_two, two, depth // 2)
     halo_k_two.start()
     for plane in range(three):
-        flat_two[plane * two : (plane + 1) * two, :] = (
-            k_two[2 + 2 * plane, 8 : 8 + two, :] + k_two[3 + 2 * plane, 8 : 8 + two, :]
+        put(
+            flat_two, plane, two,
+            k_two[2 + 2 * plane, 8 : 8 + two, :] + k_two[3 + 2 * plane, 8 : 8 + two, :],
         )
     small = paired(flat_two, depth // 4)
     gather_k.start(small[0:8] + roll(small[8:16], 64, 1))
-
-    midpoint, factor_one, factor_two = coefficients(0)
-
-    def fine_residual(block, plane):
-        total, middle = weighted(block, plane + 1, True)
-        middle = middle[8:-8]
-        applied = (8.0 / 7.0 + reaction[plane]) * middle - total * (1.0 / 56.0)
-        return refined * (source[plane] - applied), middle
-
-    halo_a.finish()
-
-    def first(plane):
-        residual, middle = fine_residual(field_a, plane)
-        step = residual * (1.0 / midpoint)
-        step_one[plane] = step
-        field_b[plane + 1, 8 : 8 + rows, :] = middle + step
-
-    each(0, planes, first)
-    halo_b.start()
     halo_b.finish()
 
-    def second(plane):
-        residual, middle = fine_residual(field_b, plane)
-        value = middle + (factor_one * step_one[plane] + factor_two * residual)
-        field_c[plane + 1, 8 : 8 + rows, :] = value
-        iterate[plane] = value
-
-    each(0, planes, second)
+    def second(start):
+        for index, (residual, middle) in enumerate(fine_residuals(field_b, start, 8)):
+            step = factor_one * step_one[start + index] + factor_two * residual
+            field_c[start + index + 1, 8 : 8 + rows, :] = middle + step
+
+    groups(0, planes, 8, second)
     halo_c.start()
+    stores[0].start()
+    halo_k_one.finish()
+    halo_k_two.finish()
+    halo_a.drain()
+    halo_k_one.drain()
     halo_c.finish()
 
-    def third(plane):
-        total = fine_residual(field_c, 2 * plane)[0] + fine_residual(field_c, 2 * plane + 1)[0]
-        flat_zero[pl.ds(pl.multiple_of(plane * rows, rows), rows), :] = total
-
-    each(0, one, third, 1)
+    def third(start):
+        values = fine_residuals(field_c, 2 * start, 8)
+        for index in range(4):
+            put(flat_zero, start + index, rows, values[2 * index][0] + values[2 * index + 1][0])
+
+    groups(0, one, 4, third)
     spread(flat_zero, f_one, one, depth)
     halo_f_one.start()
 
-    def correct(level, f, k, e, plane, mask):
+    def correct(level, f, k, e, start, count, mask):
         midpoint, factor_one, factor_two = coefficients(level)
         slope = factor_two / midpoint
         keep = (1.0 + factor_one) / midpoint + factor_two - slope * 8.0 / 7.0
-        total, middle = weighted(f, plane, False)
-        value = (keep - slope * k[plane]) * middle + (slope / 56.0) * total
-        e[plane] = value * mask
-
-    def left_over(f, k, e, plane):
-        total, middle = weighted(e, plane, False)
-        return f[plane] - ((8.0 / 7.0 + k[plane]) * middle - total * (1.0 / 56.0))
-
-    halo_k_one.finish()
-    halo_k_two.finish()
+        for index, (total, middle) in enumerate(weighted(f, start, count, False)):
+            plane = start + index
+            value = (keep - slope * k[plane]) * middle + (slope / 56.0) * total
+            e[plane] = value * mask(plane)
+
+    def left_over(f, k, e, start, count):
+        return [
+            f[start + index]
+            - ((8.0 / 7.0 + k[start + index]) * middle - total * (1.0 / 56.0))
+            for index, (total, middle) in enumerate(weighted(e, start, count, False))
+        ]
+
     gather_k.finish(k_three)
-    for level, f, k, e, exchange, out, flat, size in (
-        (1, f_one, k_one, e_one, halo_f_one, out_one, flat_one, one),
-        (2, f_two, k_two, e_two, halo_f_two, out_two, flat_two, two),
+    for plane in range(6):
+        flat_extra[32 * plane : 32 * plane + 24, :] = (
+            k_three[4 + 2 * plane] + k_three[5 + 2 * plane]
+        )
+    k_four[...] = paired(flat_extra, depth // 8).reshape(6, 16, 128)
+    halo_b.drain()
+    halo_c.drain()
+
+    for level, f, k, e, exchange, held, flat, size, spans in (
+        (1, f_one, k_one, e_one, halo_f_one, held_one, flat_one, one, (6, 4)),
+        (2, f_two, k_two, e_two, halo_f_two, held_two, flat_two, two, (10, 4)),
     ):
         extent = depth >> level
         exchange.finish()
@@ -412,61 +463,83 @@
             8 - place.agg * size, 8 + (counts[1] - place.agg) * size, f.shape[1:], extent
         )
 
-        def one_plane(plane, level=level, f=f, k=k, e=e, size=size, row_mask=row_mask):
-            at = plane_in_grid(place.box * size + plane - 2, counts[0] * size)
-            correct(level, f, k, e, plane, row_mask * at)
-
-        each(1, size + 3, one_plane)
-        out[...] = e[2 : 2 + size, 8 : 8 + size, 0:extent]
-
-        def remainder(plane, f=f, k=k, e=e, size=size, flat=flat):
-            total = left_over(f, k, e, 2 * plane + 2) + left_over(f, k, e, 2 * plane + 3)
-            flat[pl.ds(pl.multiple_of(plane * size, size), size), :] = total[8 : 8 + size]
-
-        each(0, size // 2, remainder, 1)
+        def mask(plane, size=size, row_mask=row_mask):
+            return row_mask * plane_in_grid(place.box * size + plane - 2, counts[0] * size)
+
+        def ahead(start, level=level, f=f, k=k, e=e, span=spans[0], mask=mask):
+            correct(level, f, k, e, start, span, mask)
+
+        groups(1, size + 2, spans[0], ahead)
+
+        def remainder(start, f=f, k=k, e=e, size=size, flat=flat, span=spans[1]):
+            values = left_over(f, k, e, 2 * start + 2, 2 * span)
+            for index in range(span):
+                total = values[2 * index] + values[2 * index + 1]
+                put(flat, start + index, size, total[8 : 8 + size])
+
+        groups(0, size // 2, spans[1], remainder)
         if level == 1:
             spread(flat, f_two, size // 2, extent)
             halo_f_two.start()
         else:
             small = paired(flat, extent)
             gather_f.start(small[0:8] + roll(small[8:16], 64, 1))
-
-    gather_f.finish(f_three)
+        held[...] = e[2 : 2 + size, 8 : 8 + size, 0:extent]
+        stores[level].start()
+        if level == 1:
+            halo_k_two.drain()
+            gather_k.drain()
+        else:
+            halo_f_one.drain()
+            halo_f_two.drain()
+
     mask_three = in_grid(
         8 - place.agg * three, 8 + (counts[1] - place.agg) * three, f_three.shape[1:], depth // 8
     )
-
-    def at_three(plane):
-        return mask_three * plane_in_grid(place.box * three + plane - 8, counts[0] * three)
-
-    for plane in range(3, 17):
-        correct(3, f_three, k_three, e_three, plane, at_three(plane))
-    out_three[...] = e_three[8:12, 8:12, 0 : depth // 8]
-    flat_three[...] = jnp.zeros(flat_three.shape, jnp.float32)
-    flat_extra[...] = jnp.zeros(flat_extra.shape, jnp.float32)
+    ats = {
+        plane: plane_in_grid(place.box * three + plane - 8, counts[0] * three)
+        for plane in range(3, 17)
+    }
+    gather_f.finish(f_three)
+    correct(3, f_three, k_three, e_three, 3, 14, lambda plane: mask_three * ats[plane])
+    held_three[...] = e_three[8:12, 8:12, 0 : depth // 8]
+    stores[3].start()
+    values = left_over(f_three, k_three, e_three, 4, 12)
     for plane in range(6):
-        total = jnp.zeros(f_three.shape[1:], jnp.float32)
-        for child in (4 + 2 * plane, 5 + 2 * plane):
-            total = total + left_over(f_three, k_three, e_three, child) * at_three(child)
+        total = values[2 * plane] * (mask_three * ats[4 + 2 * plane])
+        total = total + values[2 * plane + 1] * (mask_three * ats[5 + 2 * plane])
         flat_three[32 * plane : 32 * plane + 24, :] = total
-        flat_extra[32 * plane : 32 * plane + 24, :] = (
-            k_three[4 + 2 * plane] + k_three[5 + 2 * plane]
-        )
     f_four[...] = paired(flat_three, depth // 8).reshape(6, 16, 128)
-    k_four[...] = paired(flat_extra, depth // 8).reshape(6, 16, 128)
 
     four = three // 2
     mask_four = in_grid(
         4 - place.agg * four, 4 + (counts[1] - place.agg) * four, f_four.shape[1:], depth // 16
     )
-    for plane in range(1, 5):
-        at = plane_in_grid(place.box * four + plane - 2, counts[0] * four)
-        correct(4, f_four, k_four, e_four, plane, mask_four * at)
-    out_four[...] = e_four[2:4, 4:6, 0 : depth // 16]
-    for plane in (2, 3):
-        out_bottom[plane - 2] = left_over(f_four, k_four, e_four, plane)[4:6, 0 : depth // 16]
-    for exchange in exchanges:
-        exchange.drain()
+
+    def at_four(plane):
+        return mask_four * plane_in_grid(place.box * four + plane - 2, counts[0] * four)
+
+    correct(4, f_four, k_four, e_four, 1, 4, at_four)
+    held_four[...] = e_four[2:4, 4:6, 0 : depth // 16]
+    stores[4].start()
+    for index, value in enumerate(left_over(f_four, k_four, e_four, 2, 2)):
+        held_bottom[index] = value[4:6, 0 : depth // 16]
+    stores[5].start()
+    gather_f.drain()
+    for store in stores:
+        store.wait()
+
+
+def hand_on(*refs):
+    count = (len(refs) - 1) // 2
+    copies = [
+        pltpu.make_async_copy(refs[index], refs[count + index], refs[-1].at[index])
+        for index in range(count)
+    ]
+    for copy in copies:
+        copy.start()
+    for copy in copies:
+        copy.wait()
 
 
 def per_device(counts, source, guess, reaction, flags):
@@ -478,7 +551,8 @@
         return pltpu.VMEM(shape, f32)
 
     one, two = planes // 2, planes // 4
-    scratch = [vmem(planes + 2, rows + 16, depth)] * 3 + [vmem(planes, rows, depth)]
+    scratch = [pltpu.VMEM(flags.shape, jnp.int32)] + [vmem(planes, rows, depth)] * 2
+    scratch += [vmem(planes + 2, rows + 16, depth)] * 3 + [vmem(planes, rows, depth)]
     scratch += [vmem(one + 4, one + 16, 128)] * 3 + [vmem(two + 4, two + 16, 128)] * 3
     scratch += [vmem(20, 24, 128)] * 3 + [vmem(6, 16, 128)] * 3
     scratch += [vmem(one * rows, 128), vmem(two * one, 128), vmem(two // 2 * two, 128)]
@@ -486,25 +560,35 @@
     scratch += [vmem(3, 2, planes // 8, 8, 128)] * 2
     scratch += [vmem(2, 2, one // 8, 8, 128)] * 2 + [vmem(2, 2, two // 8, 8, 128)] * 2
     scratch += [vmem(7, 4, 8, 128), vmem(2, 5, 5, 8, 128)]
-    scratch += [pltpu.SemaphoreType.DMA((7, 8))] * 2 + [pltpu.SemaphoreType.DMA((2, 24))] * 2
     outs = [jax.ShapeDtypeStruct(source.shape, f32)]
     for level in range(1, LEVELS + 1):
         outs.append(
             jax.ShapeDtypeStruct((planes >> level, rows >> level, depth >> level), f32)
         )
     outs.append(outs[-1])
-    whole = pl.BlockSpec(memory_space=pltpu.VMEM)
+    scratch += [vmem(*out.shape) for out in outs[1:]]
+    scratch += [pltpu.SemaphoreType.DMA((7, 8))] * 2 + [pltpu.SemaphoreType.DMA((2, 24))] * 2
+    scratch += [pltpu.SemaphoreType.DMA((10,))]
+    anywhere = pl.BlockSpec(memory_space=pl.ANY)
+    results = pl.pallas_call(
+        functools.partial(kernel, counts),
+        out_shape=outs,
+        in_specs=[anywhere] * 4,
+        out_specs=[anywhere] * 6,
+        scratch_shapes=scratch,
+        compiler_params=pltpu.CompilerParams(
+            collective_id=0, has_side_effects=True, vmem_limit_bytes=60 * 1024 * 1024
+        ),
+    )(flags, source, guess, reaction)
     return tuple(
         pl.pallas_call(
-            functools.partial(kernel, counts),
+            hand_on,
             out_shape=outs,
-            in_specs=[pl.BlockSpec(memory_space=pltpu.SMEM)] + [whole] * 3,
-            out_specs=[whole] * 6,
-            scratch_shapes=scratch,
-            compiler_params=pltpu.CompilerParams(
-                collective_id=0, has_side_effects=True, vmem_limit_bytes=32 * 1024 * 1024
-            ),
-        )(flags, source, guess, reaction)
+            in_specs=[anywhere] * 6,
+            out_specs=[anywhere] * 6,
+            scratch_shapes=[pltpu.SemaphoreType.DMA((6,))],
+            compiler_params=pltpu.CompilerParams(vmem_limit_bytes=60 * 1024 * 1024),
+        )(*results)
     )
 
 

time: 46.3 us -> 56.1 us (1.21)
  Pallas kernels: 37.5 us -> 55 us
  local copies, waits for them, and re-layouts: 7.59 us -> 0 us
    pallas_call x0 -> x1, Pallas kernels: none -> 22.4 us  [per_device(): pl.pallas_call(hand_on, out_shape=outs, in_specs=[anywhere] * 6, out_spec...]
    unnamed x14 -> x0, local copies, waits for them, and re-layouts: 7.59 us -> none
    pallas_call x1, Pallas kernels: 37.5 us -> 32.6 us  [per_device(): pl.pallas_call(functools.partial(kernel, counts), out_shape=outs, in_spec...]
where the time goes in v2:
time: 56.1 us; the launch traced here: 55.6 us
  Pallas kernels  55 us (98%)
  between operations  0.64 us (1%)
    pallas_call x1, Pallas kernels, per_device(): pl.pallas_call(functools.partial(kernel, counts), out_shape=outs, in_spec...  32.6 us
    pallas_call x1, Pallas kernels, per_device(): pl.pallas_call(hand_on, out_shape=outs, in_specs=[anywhere] * 6, out_spec...  22.4 us

profile of v2, /device:TPU:1, one launch (start us, length us, event | category | flops | bytes accessed | tf_op | source)
XLA Modules:
  0.0 55.6 jit_solution(12546771141330896266)
XLA Ops:
  0.6 32.6 %shard_map.91 = (f32[32,32,128]{2,1,0:T(8,128)}, f32[16,16,64]{2,1,0:T(8,128)}, f32[8,8,32]{2,1,0:T(8,128)}, f32[4,4,16]{2,1,0:T(4,128)}, f32[2,2,8]{2,1,0:T(2,128)}, /*index=5*/f32[2,2,8]{2,1,0:T(2,128)}) custom-call(s32[1,1,4]{2,1,0:T(1,128)} %flags_in.1, f32[32,32,128]{2,1,0:T(8,128)} %source_in.1, f32[32,32,128]{2,1,0:T(8,128)} %guess_in.1, ...), custom_call_target="tpu_custom_call" | custom-call | tf_op jit(solution)/shard_map/pallas_call | solution.py:573
  33.2 22.4 %shard_map.92 = (f32[32,32,128]{2,1,0:T(8,128)}, f32[16,16,64]{2,1,0:T(8,128)}, f32[8,8,32]{2,1,0:T(8,128)}, f32[4,4,16]{2,1,0:T(4,128)}, f32[2,2,8]{2,1,0:T(2,128)}, /*index=5*/f32[2,2,8]{2,1,0:T(2,128)}) custom-call(f32[32,32,128]{2,1,0:T(8,128)} %get-tuple-element.12.refs_0_, f32[16,16,64]{2,1,0:T(8,128)} %get-tuple-element.13.refs_1_, ...), custom_call_target="tpu_custom_call" | custom-call | tf_op jit(solution)/shard_map/pallas_call | solution.py:584

commit v3 on v2

--- a/solution.py
+++ b/solution.py
@@ -151,6 +151,70 @@
             pl.when(self.place.has(dx, dy))(lambda n=number: self.copy(n).wait_send())
 
 
+class FineHalo(Halo):
+    def __init__(self, place, block, packs, sides, corners, outer, send, recv):
+        super().__init__(place, block, 1, packs, sides, corners, send, recv)
+        self.outer = outer
+
+    def clear(self):
+        planes, rows = self.planes, self.rows
+        edge = jnp.zeros((1,) + self.block.shape[1:], jnp.float32)
+        self.block[0:1] = edge
+        self.block[planes + 1 : planes + 2] = edge
+        strip = jnp.zeros((planes + 2, 8, 128), jnp.float32)
+        self.block[:, 0:8, :] = strip
+        self.block[:, 8 + rows : 16 + rows, :] = strip
+        for ref in (self.sides, self.corners, self.outer):
+            ref[...] = jnp.zeros(ref.shape, jnp.float32)
+
+    def copy(self, number):
+        dx, dy = NEAR[number]
+        if dy != 0:
+            return super().copy(number)
+        plane = self.planes if dx > 0 else 1
+        return pltpu.make_async_remote_copy(
+            src_ref=self.block.at[plane, 8 : 8 + self.rows],
+            dst_ref=self.outer.at[0 if dx > 0 else 1, 8 : 8 + self.rows],
+            send_sem=self.send.at[number],
+            recv_sem=self.recv.at[number],
+            device_id=self.place.device(dx, dy),
+            device_id_type=MESH,
+        )
+
+    def finish(self, refined, scale):
+        planes, rows = self.planes, self.rows
+        for number, (dx, dy) in enumerate(NEAR):
+            pl.when(self.place.has(-dx, -dy))(lambda n=number: self.copy(n).wait_recv())
+        factor = refined * scale
+        sides, ends = [], []
+        for side in (0, 1):
+            strip = self.sides[side].reshape(planes, 128)
+            at = row_ids(strip.shape)
+            before = jnp.where(at == 0, 0.0, roll(strip, 1, 0))
+            after = jnp.where(at == planes - 1, 0.0, roll(strip, -1, 0))
+            sides.append(factor * along_lanes((before + after) + (strip + strip), True))
+        for end in (0, 1):
+            slot = 7 if end == 0 else 0
+            low, high = self.corners[2 * end], self.corners[2 * end + 1]
+            plane = jnp.concatenate(
+                [
+                    unpacked(low, slot, 1, True),
+                    self.outer[end, 8 : 8 + rows, :],
+                    unpacked(high, slot, 1, False),
+                ],
+                axis=0,
+            )
+            total = (roll(plane, 1, 0) + roll(plane, -1, 0)) + (plane + plane)
+            ends.append(factor * along_lanes(total[8 : 8 + rows], True))
+        return sides, ends
+
+
+def edge_tile(strip, plane, last):
+    base = plane // 8 * 8
+    value = roll(strip[base : base + 8], (7 if last else 0) - plane % 8, 0)
+    return jnp.where(row_ids((8, 128)) == (7 if last else 0), value, 0.0)
+
+
 class Gather:
     def __init__(self, place, tiles, send, recv):
         self.place, self.tiles, self.send, self.recv = place, tiles, send, recv
@@ -225,6 +289,15 @@
         pl.semaphore_wait(semaphore, spans[0] * spans[1] - 1)
 
 
+def along_lanes(total, wrap):
+    left, right = roll(total, 1, 1), roll(total, -1, 1)
+    if wrap:
+        lanes = lane_ids(total.shape)
+        left = jnp.where(lanes == 0, 0.0, left)
+        right = jnp.where(lanes == 127, 0.0, right)
+    return (left + right) + (total + total)
+
+
 def weighted(block, start, count, wrap):
     held = [block[start - 1 + index] for index in range(count + 2)]
     pairs = [low + high for low, high in zip(held[:-1], held[1:])]
@@ -235,25 +308,24 @@
         middle = held[index + 1]
         if wrap:
             total, middle = total[8:-8], middle[8:-8]
-            lanes = lane_ids(total.shape)
-            left = jnp.where(lanes == 0, 0.0, roll(total, 1, 1))
-            right = jnp.where(lanes == 127, 0.0, roll(total, -1, 1))
-        else:
-            left, right = roll(total, 1, 1), roll(total, -1, 1)
-        results.append(((left + right) + (total + total), middle))
+        results.append((along_lanes(total, wrap), middle))
     return results
 
 
-def paired(flat, extent):
+def pair_matrix(extent):
+    source, target = row_ids((256, 128)) % 128, lane_ids((256, 128))
+    pairs = (source < extent) & ((source == 2 * target) | (source == 2 * target + 1))
+    return jnp.where(pairs, 0.5, 0.0).astype(jnp.bfloat16)
+
+
+def paired(flat, matrix):
     half = flat.shape[0] // 2
     rows = flat[pl.ds(0, half, stride=2), :] + flat[pl.ds(1, half, stride=2), :]
     high = rows.astype(jnp.bfloat16)
     low = (rows - high.astype(jnp.float32)).astype(jnp.bfloat16)
-    source, target = row_ids((256, 128)) % 128, lane_ids((256, 128))
-    pairs = (source < extent) & ((source == 2 * target) | (source == 2 * target + 1))
     return jnp.dot(
         jnp.concatenate([high, low], axis=1),
-        jnp.where(pairs, 0.5, 0.0).astype(jnp.bfloat16),
+        matrix[...],
         preferred_element_type=jnp.float32,
     )
 
@@ -285,7 +357,7 @@
     flags_in, source_in, guess_in, reaction_in,
     iterate, out_one, out_two, out_three, out_four, out_bottom,
     flags, source, reaction,
-    field_a, field_b, field_c, step_one,
+    field_a, field_b, field_c, outer, matrices,
     f_one, k_one, e_one, f_two, k_two, e_two,
     f_three, k_three, e_three, f_four, k_four, e_four,
     flat_zero, flat_one, flat_two, flat_three, flat_extra,
@@ -302,9 +374,13 @@
             near_send.at[number], near_recv.at[number],
         )
 
-    halo_a = halo(0, field_a, 1, packs_zero, sides_zero, 0)
-    halo_b = halo(1, field_b, 1, packs_zero, sides_zero, 1)
-    halo_c = halo(2, field_c, 1, packs_zero, sides_zero, 2)
+    halo_a, halo_b, halo_c = (
+        FineHalo(
+            place, block, packs_zero.at[index], sides_zero.at[index], corners.at[index],
+            outer.at[index], near_send.at[index], near_recv.at[index],
+        )
+        for index, block in enumerate((field_a, field_b, field_c))
+    )
     halo_f_one = halo(3, f_one, 2, packs_one, sides_one, 0)
     halo_k_one = halo(4, k_one, 2, packs_one, sides_one, 1)
     halo_f_two = halo(5, f_two, 2, packs_two, sides_two, 0)
@@ -336,12 +412,14 @@
         exchange.clear()
     flat_three[...] = jnp.zeros(flat_three.shape, jnp.float32)
     flat_extra[...] = jnp.zeros(flat_extra.shape, jnp.float32)
+    for level in range(LEVELS):
+        matrices[level] = pair_matrix(depth >> level)
     place.barrier()
     loads[0].wait()
     halo_a.start()
 
-    def spread(flat, target, count, extent):
-        values = paired(flat, extent)
+    def spread(flat, target, count, level):
+        values = paired(flat, matrices.at[level])
         target[2 : 2 + count, 8 : 8 + count, :] = values.reshape(count, count, 128)
 
     def put(flat, plane, size, value):
@@ -356,7 +434,7 @@
             put(flat_zero, at, rows, reaction[2 * at] + reaction[2 * at + 1])
 
     groups(0, one, 4, coarse_reaction)
-    spread(flat_zero, k_one, one, depth)
+    spread(flat_zero, k_one, one, 0)
     halo_k_one.start()
     loads[2].wait()
     loads[3].wait()
@@ -378,55 +456,69 @@
             results.append((refined * (source[start + index] - applied), middle))
         return results
 
-    halo_a.finish()
+    def add_edges(block, shares):
+        (low, high), ends = shares
+        for plane in range(planes):
+            block[plane + 1, 8:16, :] += edge_tile(low, plane, False)
+            block[plane + 1, rows : 8 + rows, :] += edge_tile(high, plane, True)
+        block[1, 8 : 8 + rows, :] += ends[0]
+        block[planes, 8 : 8 + rows, :] += ends[1]
 
     def first(start):
         for index, (residual, middle) in enumerate(fine_residuals(field_a, start, 8)):
-            step = residual * (1.0 / midpoint)
-            step_one[start + index] = step
-            field_b[start + index + 1, 8 : 8 + rows, :] = middle + step
+            field_b[start + index + 1, 8 : 8 + rows, :] = middle + residual * (1.0 / midpoint)
 
     groups(0, planes, 8, first)
+    add_edges(field_b, halo_a.finish(refined, 1.0 / (56.0 * midpoint)))
     halo_b.start()
+
+    def second(start):
+        for index, (residual, middle) in enumerate(fine_residuals(field_b, start, 8)):
+            before = field_a[start + index + 1, 8 : 8 + rows, :]
+            step = factor_one * (middle - before) + factor_two * residual
+            field_c[start + index + 1, 8 : 8 + rows, :] = middle + step
+
+    groups(0, planes, 8, second)
+    halo_a.drain()
+    add_edges(field_c, halo_b.finish(refined, factor_two / 56.0))
+    halo_c.start()
+    stores[0].start()
+
+    def third(start):
+        values = fine_residuals(field_c, 2 * start, 8)
+        for index in range(4):
+            put(flat_zero, start + index, rows, values[2 * index][0] + values[2 * index + 1][0])
+
+    groups(0, one, 4, third)
+    halo_b.drain()
+    halo_k_one.drain()
+    (low, high), ends = halo_c.finish(refined, 1.0 / 56.0)
+    for plane in range(one):
+        at = plane * rows
+        for strip, last, begin in ((low, False, at), (high, True, at + rows - 8)):
+            both = edge_tile(strip, 2 * plane, last) + edge_tile(strip, 2 * plane + 1, last)
+            flat_zero[begin : begin + 8, :] += both
+    flat_zero[0:rows, :] += ends[0]
+    flat_zero[(one - 1) * rows : one * rows, :] += ends[1]
+    spread(flat_zero, f_one, one, 0)
+    halo_f_one.start()
 
     for plane in range(two):
         put(
             flat_one, plane, one,
             k_one[2 + 2 * plane, 8 : 8 + one, :] + k_one[3 + 2 * plane, 8 : 8 + one, :],
         )
-    spread(flat_one, k_two, two, depth // 2)
+    spread(flat_one, k_two, two, 1)
     halo_k_two.start()
     for plane in range(three):
         put(
             flat_two, plane, two,
             k_two[2 + 2 * plane, 8 : 8 + two, :] + k_two[3 + 2 * plane, 8 : 8 + two, :],
         )
-    small = paired(flat_two, depth // 4)
+    small = paired(flat_two, matrices.at[2])
     gather_k.start(small[0:8] + roll(small[8:16], 64, 1))
-    halo_b.finish()
-
-    def second(start):
-        for index, (residual, middle) in enumerate(fine_residuals(field_b, start, 8)):
-            step = factor_one * step_one[start + index] + factor_two * residual
-            field_c[start + index + 1, 8 : 8 + rows, :] = middle + step
-
-    groups(0, planes, 8, second)
-    halo_c.start()
-    stores[0].start()
     halo_k_one.finish()
-    halo_k_two.finish()
-    halo_a.drain()
-    halo_k_one.drain()
-    halo_c.finish()
-
-    def third(start):
-        values = fine_residuals(field_c, 2 * start, 8)
-        for index in range(4):
-            put(flat_zero, start + index, rows, values[2 * index][0] + values[2 * index + 1][0])
-
-    groups(0, one, 4, third)
-    spread(flat_zero, f_one, one, depth)
-    halo_f_one.start()
+    halo_c.drain()
 
     def correct(level, f, k, e, start, count, mask):
         midpoint, factor_one, factor_two = coefficients(level)
@@ -444,15 +536,6 @@
             for index, (total, middle) in enumerate(weighted(e, start, count, False))
         ]
 
-    gather_k.finish(k_three)
-    for plane in range(6):
-        flat_extra[32 * plane : 32 * plane + 24, :] = (
-            k_three[4 + 2 * plane] + k_three[5 + 2 * plane]
-        )
-    k_four[...] = paired(flat_extra, depth // 8).reshape(6, 16, 128)
-    halo_b.drain()
-    halo_c.drain()
-
     for level, f, k, e, exchange, held, flat, size, spans in (
         (1, f_one, k_one, e_one, halo_f_one, held_one, flat_one, one, (6, 4)),
         (2, f_two, k_two, e_two, halo_f_two, held_two, flat_two, two, (10, 4)),
@@ -479,10 +562,11 @@
 
         groups(0, size // 2, spans[1], remainder)
         if level == 1:
-            spread(flat, f_two, size // 2, extent)
+            spread(flat, f_two, size // 2, level)
             halo_f_two.start()
+            halo_k_two.finish()
         else:
-            small = paired(flat, extent)
+            small = paired(flat, matrices.at[level])
             gather_f.start(small[0:8] + roll(small[8:16], 64, 1))
         held[...] = e[2 : 2 + size, 8 : 8 + size, 0:extent]
         stores[level].start()
@@ -492,6 +576,13 @@
         else:
             halo_f_one.drain()
             halo_f_two.drain()
+
+    gather_k.finish(k_three)
+    for plane in range(6):
+        flat_extra[32 * plane : 32 * plane + 24, :] = (
+            k_three[4 + 2 * plane] + k_three[5 + 2 * plane]
+        )
+    k_four[...] = paired(flat_extra, matrices.at[3]).reshape(6, 16, 128)
 
     mask_three = in_grid(
         8 - place.agg * three, 8 + (counts[1] - place.agg) * three, f_three.shape[1:], depth // 8
@@ -509,7 +600,7 @@
         total = values[2 * plane] * (mask_three * ats[4 + 2 * plane])
         total = total + values[2 * plane + 1] * (mask_three * ats[5 + 2 * plane])
         flat_three[32 * plane : 32 * plane + 24, :] = total
-    f_four[...] = paired(flat_three, depth // 8).reshape(6, 16, 128)
+    f_four[...] = paired(flat_three, matrices.at[3]).reshape(6, 16, 128)
 
     four = three // 2
     mask_four = in_grid(
@@ -531,14 +622,26 @@
 
 
 def hand_on(*refs):
-    count = (len(refs) - 1) // 2
-    copies = [
-        pltpu.make_async_copy(refs[index], refs[count + index], refs[-1].at[index])
-        for index in range(count)
-    ]
-    for copy in copies:
+    sources, targets, held = refs[0:6], refs[6:12], refs[12:18]
+    semaphores = refs[18]
+    size = sources[0].shape[0] // 4
+    parts = [(0, pl.ds(piece * size, size)) for piece in range(4)]
+    parts += [(index, pl.ds(0, sources[index].shape[0])) for index in range(1, 6)]
+    inward, outward = [], []
+    for number, (index, part) in enumerate(parts):
+        inner = held[index].at[part]
+        inward.append(
+            pltpu.make_async_copy(sources[index].at[part], inner, semaphores.at[0, number])
+        )
+        outward.append(
+            pltpu.make_async_copy(inner, targets[index].at[part], semaphores.at[1, number])
+        )
+    for copy in inward:
         copy.start()
-    for copy in copies:
+    for before, after in zip(inward, outward):
+        before.wait()
+        after.start()
+    for copy in outward:
         copy.wait()
 
 
@@ -552,7 +655,8 @@
 
     one, two = planes // 2, planes // 4
     scratch = [pltpu.VMEM(flags.shape, jnp.int32)] + [vmem(planes, rows, depth)] * 2
-    scratch += [vmem(planes + 2, rows + 16, depth)] * 3 + [vmem(planes, rows, depth)]
+    scratch += [vmem(planes + 2, rows + 16, depth)] * 3 + [vmem(3, 2, rows + 16, depth)]
+    scratch += [pltpu.VMEM((LEVELS, 256, 128), jnp.bfloat16)]
     scratch += [vmem(one + 4, one + 16, 128)] * 3 + [vmem(two + 4, two + 16, 128)] * 3
     scratch += [vmem(20, 24, 128)] * 3 + [vmem(6, 16, 128)] * 3
     scratch += [vmem(one * rows, 128), vmem(two * one, 128), vmem(two // 2 * two, 128)]
@@ -586,7 +690,7 @@
             out_shape=outs,
             in_specs=[anywhere] * 6,
             out_specs=[anywhere] * 6,
-            scratch_shapes=[pltpu.SemaphoreType.DMA((6,))],
+            scratch_shapes=[vmem(*out.shape) for out in outs] + [pltpu.SemaphoreType.DMA((2, 9))],
             compiler_params=pltpu.CompilerParams(vmem_limit_bytes=60 * 1024 * 1024),
         )(*results)
     )

time: 56.1 us -> 33.7 us (0.60)
  Pallas kernels: 55 us -> 32.7 us
    pallas_call x1, Pallas kernels: 22.4 us -> 1.99 us  [per_device(): pl.pallas_call(hand_on, out_shape=outs, in_specs=[anywhere] * 6, out_spec...]
    pallas_call x1, Pallas kernels: 32.6 us -> 30.7 us  [per_device(): pl.pallas_call(functools.partial(kernel, counts), out_shape=outs, in_spec...]
where the time goes in v3:
time: 33.7 us; the launch traced here: 33.4 us
  Pallas kernels  32.7 us (97%)
  between operations  0.64 us (2%)
    pallas_call x1, Pallas kernels, per_device(): pl.pallas_call(functools.partial(kernel, counts), out_shape=outs, in_spec...  30.7 us
    pallas_call x1, Pallas kernels, per_device(): pl.pallas_call(hand_on, out_shape=outs, in_specs=[anywhere] * 6, out_spec...  1.99 us

profile of v3, /device:TPU:1, one launch (start us, length us, event | category | flops | bytes accessed | tf_op | source)
XLA Modules:
  0.0 33.4 jit_solution(9271599250724193368)
XLA Ops:
  0.6 30.7 %shard_map.91 = (f32[32,32,128]{2,1,0:T(8,128)}, f32[16,16,64]{2,1,0:T(8,128)}, f32[8,8,32]{2,1,0:T(8,128)}, f32[4,4,16]{2,1,0:T(4,128)}, f32[2,2,8]{2,1,0:T(2,128)}, /*index=5*/f32[2,2,8]{2,1,0:T(2,128)}) custom-call(s32[1,1,4]{2,1,0:T(1,128)} %flags_in.1, f32[32,32,128]{2,1,0:T(8,128)} %source_in.1, f32[32,32,128]{2,1,0:T(8,128)} %guess_in.1, ...), custom_call_target="tpu_custom_call" | custom-call | tf_op jit(solution)/shard_map/pallas_call | solution.py:677
  31.4 2.0 %shard_map.92 = (f32[32,32,128]{2,1,0:T(8,128)}, f32[16,16,64]{2,1,0:T(8,128)}, f32[8,8,32]{2,1,0:T(8,128)}, f32[4,4,16]{2,1,0:T(4,128)}, f32[2,2,8]{2,1,0:T(2,128)}, /*index=5*/f32[2,2,8]{2,1,0:T(2,128)}) custom-call(f32[32,32,128]{2,1,0:T(8,128)} %get-tuple-element.12.refs_0_, f32[16,16,64]{2,1,0:T(8,128)} %get-tuple-element.13.refs_1_, ...), custom_call_target="tpu_custom_call" | custom-call | tf_op jit(solution)/shard_map/pallas_call | solution.py:688

commit v4 on v3

--- a/solution.py
+++ b/solution.py
@@ -10,7 +10,6 @@
 LEVELS = 4
 MESH = pl.DeviceIdType.MESH
 NEAR = [(dx, dy) for dx in (-1, 0, 1) for dy in (-1, 0, 1) if (dx, dy) != (0, 0)]
-WIDE = [(dx, dy) for dx in range(-2, 3) for dy in range(-2, 3) if (dx, dy) != (0, 0)]
 
 
 def coefficients(level_index):
@@ -63,6 +62,42 @@
     if width > 1:
         mask = mask & (lanes < 64)
     return jnp.where(mask, value, 0.0)
+
+
+def pack_edges(block, width, high, low):
+    planes, rows = block.shape[0] - 2 * width, block.shape[1] - 16
+    for tile in range(planes // 8):
+        upper = jnp.zeros((8, 128), jnp.float32)
+        lower = upper
+        for slot in range(8):
+            row, half = slot_place(slot, width)
+            mask = slot_mask(slot, width)
+            plane = width + 8 * tile + slot
+            last = roll(block[plane, rows : rows + 8, :], row + width - 8, 0)
+            first = roll(block[plane, 8:16, :], row, 0)
+            if half:
+                last, first = roll(last, 64, 1), roll(first, 64, 1)
+            upper = jnp.where(mask, last, upper)
+            lower = jnp.where(mask, first, lower)
+        high[tile] = upper
+        low[tile] = lower
+
+
+def unpack_edges(block, width, tile, low, high):
+    rows = block.shape[1] - 16
+    for slot in range(8):
+        plane = width + 8 * tile + slot
+        block[plane, 0:8, :] = unpacked(low, slot, width, True)
+        block[plane, rows + 8 : rows + 16, :] = unpacked(high, slot, width, False)
+
+
+def unpack_corners(block, width, side, low, high):
+    planes, rows = block.shape[0] - 2 * width, block.shape[1] - 16
+    for index in range(width):
+        slot = 8 - width + index if side == 0 else index
+        plane = index if side == 0 else planes + width + index
+        block[plane, 0:8, :] = unpacked(low, slot, width, True)
+        block[plane, rows + 8 : rows + 16, :] = unpacked(high, slot, width, False)
 
 
 class Halo:
@@ -105,46 +140,25 @@
         )
 
     def start(self):
-        w, rows = self.width, self.rows
         for number, (dx, dy) in enumerate(NEAR):
             if dy == 0:
                 pl.when(self.place.has(dx, dy))(lambda n=number: self.copy(n).start())
-        for tile in range(self.planes // 8):
-            high = jnp.zeros((8, 128), jnp.float32)
-            low = high
-            for slot in range(8):
-                row, half = slot_place(slot, w)
-                mask = slot_mask(slot, w)
-                plane = w + 8 * tile + slot
-                last = roll(self.block[plane, rows : rows + 8, :], row + w - 8, 0)
-                first = roll(self.block[plane, 8:16, :], row, 0)
-                if half:
-                    last, first = roll(last, 64, 1), roll(first, 64, 1)
-                high = jnp.where(mask, last, high)
-                low = jnp.where(mask, first, low)
-            self.packs[0, tile] = high
-            self.packs[1, tile] = low
+        pack_edges(self.block, self.width, self.packs.at[0], self.packs.at[1])
         for number, (dx, dy) in enumerate(NEAR):
             if dy != 0:
                 pl.when(self.place.has(dx, dy))(lambda n=number: self.copy(n).start())
 
     def finish(self):
-        w, planes, rows = self.width, self.planes, self.rows
+        self.arrive()
+        for tile in range(self.planes // 8):
+            unpack_edges(self.block, self.width, tile, self.sides[0, tile], self.sides[1, tile])
+        for side in (0, 1):
+            low, high = self.corners[2 * side], self.corners[2 * side + 1]
+            unpack_corners(self.block, self.width, side, low, high)
+
+    def arrive(self):
         for number, (dx, dy) in enumerate(NEAR):
             pl.when(self.place.has(-dx, -dy))(lambda n=number: self.copy(n).wait_recv())
-        for tile in range(planes // 8):
-            low, high = self.sides[0, tile], self.sides[1, tile]
-            for slot in range(8):
-                plane = w + 8 * tile + slot
-                self.block[plane, 0:8, :] = unpacked(low, slot, w, True)
-                self.block[plane, rows + 8 : rows + 16, :] = unpacked(high, slot, w, False)
-        for side in (0, 1):
-            low, high = self.corners[2 * side], self.corners[2 * side + 1]
-            for index in range(w):
-                slot = 8 - w + index if side == 0 else index
-                plane = index if side == 0 else planes + w + index
-                self.block[plane, 0:8, :] = unpacked(low, slot, w, True)
-                self.block[plane, rows + 8 : rows + 16, :] = unpacked(high, slot, w, False)
 
     def drain(self):
         for number, (dx, dy) in enumerate(NEAR):
@@ -215,18 +229,28 @@
     return jnp.where(row_ids((8, 128)) == (7 if last else 0), value, 0.0)
 
 
-class Gather:
-    def __init__(self, place, tiles, send, recv):
-        self.place, self.tiles, self.send, self.recv = place, tiles, send, recv
+class Coefficients(Halo):
+    def __init__(self, place, fields, packs, ends, sides, corners, outer, send, recv):
+        self.place, self.fields = place, fields
+        self.packs, self.ends = packs, ends
+        self.sides, self.corners, self.outer = sides, corners, outer
+        self.send, self.recv = send, recv
 
     def clear(self):
-        self.tiles[...] = jnp.zeros(self.tiles.shape, jnp.float32)
+        for ref in (self.sides, self.corners, self.outer):
+            ref[...] = jnp.zeros(ref.shape, jnp.float32)
 
     def copy(self, number):
-        dx, dy = WIDE[number]
+        dx, dy = NEAR[number]
+        across, along = (0 if dx > 0 else 1), (0 if dy > 0 else 1)
+        if dy == 0:
+            source, target = self.ends.at[across], self.outer.at[across]
+        else:
+            source = self.packs.at[along]
+            target = self.sides.at[along] if dx == 0 else self.corners.at[2 * across + along]
         return pltpu.make_async_remote_copy(
-            src_ref=self.tiles.at[2, 2],
-            dst_ref=self.tiles.at[2 - dx, 2 - dy],
+            src_ref=source,
+            dst_ref=target,
             send_sem=self.send.at[number],
             recv_sem=self.recv.at[number],
             device_id=self.place.device(dx, dy),
@@ -234,31 +258,91 @@
         )
 
     def start(self, tile):
-        self.tiles[2, 2] = tile
-        for number, (dx, dy) in enumerate(WIDE):
+        self.tile = tile
+        at = 0
+        for block in self.fields:
+            size = (block.shape[0] - 4) // 8
+            part = pl.ds(at, size)
+            pack_edges(block, 2, self.packs.at[0, part], self.packs.at[1, part])
+            at += size
+        at = 0
+        for block in self.fields:
+            planes, rows = block.shape[0] - 4, block.shape[1] - 16
+            size = rows // 8
+            for index in range(2):
+                for across, plane in ((0, planes + index), (1, 2 + index)):
+                    value = block[plane, 8 : 8 + rows, :].reshape(size, 8, 128)
+                    self.ends[across, at : at + size] = value
+                at += size
+        for ref in (self.packs, self.ends):
+            for index in range(2):
+                ref[index, ref.shape[1] - 1] = tile
+        for number, (dx, dy) in enumerate(NEAR):
             pl.when(self.place.has(dx, dy))(lambda n=number: self.copy(n).start())
 
-    def finish(self, field):
-        for number, (dx, dy) in enumerate(WIDE):
-            pl.when(self.place.has(-dx, -dy))(lambda n=number: self.copy(n).wait_recv())
-        field[...] = jnp.zeros(field.shape, jnp.float32)
-        rows, lanes = row_ids((8, 128)), lane_ids((8, 128))
-        for bx in range(5):
-            for group in range(3):
-                pair = [self.tiles[bx, by] for by in range(2 * group, min(2 * group + 2, 5))]
-                for index in range(4):
-                    total = jnp.zeros((8, 128), jnp.float32)
-                    for where, tile in enumerate(pair):
-                        value = roll(tile, 4 * where - 4 * (index % 2), 0)
-                        if index >= 2:
-                            value = roll(value, 64, 1)
-                        mask = (rows >= 4 * where) & (rows < 4 * where + 4) & (lanes < 64)
-                        total = jnp.where(mask, value, total)
-                    field[4 * bx + index, 8 * group : 8 * group + 8, :] = total
-
-    def drain(self):
-        for number, (dx, dy) in enumerate(WIDE):
-            pl.when(self.place.has(dx, dy))(lambda n=number: self.copy(n).wait_send())
+    def finish(self, third):
+        self.arrive()
+        at, end = 0, 0
+        for block in self.fields:
+            planes, rows = block.shape[0] - 4, block.shape[1] - 16
+            count, size = planes // 8, rows // 8
+            for tile in range(count):
+                low, high = self.sides[0, at + tile], self.sides[1, at + tile]
+                unpack_edges(block, 2, tile, low, high)
+            for side in (0, 1):
+                tile = at + (count - 1 if side == 0 else 0)
+                low, high = self.corners[2 * side, tile], self.corners[2 * side + 1, tile]
+                unpack_corners(block, 2, side, low, high)
+                for index in range(2):
+                    plane = index if side == 0 else planes + 2 + index
+                    first = end + index * size
+                    value = self.outer[side, first : first + size].reshape(rows, 128)
+                    block[plane, 8 : 8 + rows, :] = value
+            at += count
+            end += 2 * size
+        around = [
+            [self.corners[0, at], self.outer[0, end], self.corners[1, at]],
+            [self.sides[0, at], self.tile, self.sides[1, at]],
+            [self.corners[2, at], self.outer[1, end], self.corners[3, at]],
+        ]
+        lay_out(around, third)
+
+
+def lay_out(around, field):
+    rows, lanes = row_ids((8, 128)), lane_ids((8, 128))
+    for bx in range(3):
+        for index in range(4):
+            values = []
+            for by in range(3):
+                value = roll(around[bx][by], 4 * (by % 2) - 4 * (index % 2), 0)
+                values.append(roll(value, 64, 1) if index >= 2 else value)
+            head = jnp.where(rows < 4, values[0], values[1])
+            tail = jnp.where(rows < 4, values[2], 0.0)
+            field[4 * bx + index, 0:8, :] = jnp.where(lanes < 64, head, 0.0)
+            field[4 * bx + index, 8:16, :] = jnp.where(lanes < 64, tail, 0.0)
+
+
+class Gather(Halo):
+    def __init__(self, place, tiles, send, recv):
+        self.place, self.tiles, self.send, self.recv = place, tiles, send, recv
+
+    def clear(self):
+        self.tiles[...] = jnp.zeros(self.tiles.shape, jnp.float32)
+
+    def copy(self, number):
+        dx, dy = NEAR[number]
+        return pltpu.make_async_remote_copy(
+            src_ref=self.tiles.at[1, 1],
+            dst_ref=self.tiles.at[1 - dx, 1 - dy],
+            send_sem=self.send.at[number],
+            recv_sem=self.recv.at[number],
+            device_id=self.place.device(dx, dy),
+            device_id_type=MESH,
+        )
+
+    def start(self):
+        for number, (dx, dy) in enumerate(NEAR):
+            pl.when(self.place.has(dx, dy))(lambda n=number: self.copy(n).start())
 
 
 class Place:
@@ -273,9 +357,9 @@
         x, y = self.device(dx, dy)
         return (x >= 0) & (x < self.counts[0]) & (y >= 0) & (y < self.counts[1])
 
-    def barrier(self):
+    def greet(self):
         semaphore = pltpu.get_barrier_semaphore()
-        for dx, dy in WIDE:
+        for dx, dy in NEAR:
 
             @pl.when(self.has(dx, dy))
             def _(dx=dx, dy=dy):
@@ -283,10 +367,11 @@
                     semaphore, inc=1, device_id=self.device(dx, dy), device_id_type=MESH
                 )
 
+    def await_greetings(self):
         spans = []
         for at, count in zip((self.box, self.agg), self.counts):
-            spans.append(1 + jnp.minimum(at, 2) + jnp.minimum(count - 1 - at, 2))
-        pl.semaphore_wait(semaphore, spans[0] * spans[1] - 1)
+            spans.append(1 + jnp.minimum(at, 1) + jnp.minimum(count - 1 - at, 1))
+        pl.semaphore_wait(pltpu.get_barrier_semaphore(), spans[0] * spans[1] - 1)
 
 
 def along_lanes(total, wrap):
@@ -362,8 +447,8 @@
     f_three, k_three, e_three, f_four, k_four, e_four,
     flat_zero, flat_one, flat_two, flat_three, flat_extra,
     packs_zero, sides_zero, packs_one, sides_one, packs_two, sides_two, corners,
-    tiles, held_one, held_two, held_three, held_four, held_bottom,
-    near_send, near_recv, wide_send, wide_recv, local,
+    k_packs, k_ends, k_sides, k_corners, k_outer, tiles_three, tiles_four, held_one, held_two, held_three, held_four, held_bottom,
+    near_send, near_recv, local,
 ):
     place = Place(counts)
     planes, rows, depth = source.shape
@@ -382,21 +467,27 @@
         for index, block in enumerate((field_a, field_b, field_c))
     )
     halo_f_one = halo(3, f_one, 2, packs_one, sides_one, 0)
-    halo_k_one = halo(4, k_one, 2, packs_one, sides_one, 1)
-    halo_f_two = halo(5, f_two, 2, packs_two, sides_two, 0)
-    halo_k_two = halo(6, k_two, 2, packs_two, sides_two, 1)
-    gather_f = Gather(place, tiles.at[0], wide_send.at[0], wide_recv.at[0])
-    gather_k = Gather(place, tiles.at[1], wide_send.at[1], wide_recv.at[1])
+    halo_f_two = halo(4, f_two, 2, packs_two, sides_two, 0)
+    halo_k = Coefficients(
+        place, (k_one, k_two), k_packs, k_ends, k_sides, k_corners, k_outer,
+        near_send.at[5], near_recv.at[5],
+    )
+    gather_three = Gather(place, tiles_three, near_send.at[6], near_recv.at[6])
+    gather_four = Gather(place, tiles_four, near_send.at[7], near_recv.at[7])
     own_a = field_a.at[1 : 1 + planes, 8 : 8 + rows]
     own_c = field_c.at[1 : 1 + planes, 8 : 8 + rows]
+    quarter = planes // 4
+    parts = [pl.ds(index * quarter, quarter) for index in range(4)]
+    pairs = [(guess_in.at[part], own_a.at[part]) for part in parts]
+    pairs += [(flags_in, flags)]
+    pairs += [(reaction_in.at[part], reaction.at[part]) for part in parts]
+    pairs += [(source_in.at[part], source.at[part]) for part in parts]
     loads = [
-        pltpu.make_async_copy(origin, target, local.at[index])
-        for index, (origin, target) in enumerate(
-            ((guess_in, own_a), (reaction_in, reaction), (source_in, source), (flags_in, flags))
-        )
+        pltpu.make_async_copy(origin, target, local.at[6 + index])
+        for index, (origin, target) in enumerate(pairs)
     ]
     stores = [
-        pltpu.make_async_copy(origin, target, local.at[4 + index])
+        pltpu.make_async_copy(origin, target, local.at[index])
         for index, (origin, target) in enumerate(
             (
                 (own_c, iterate), (held_one, out_one), (held_two, out_two),
@@ -404,18 +495,20 @@
             )
         )
     ]
-    for load in loads:
+    for load in loads[:4]:
         load.start()
     for exchange in (
-        halo_a, halo_b, halo_c, halo_f_one, halo_k_one, halo_f_two, halo_k_two, gather_f, gather_k,
+        halo_a, halo_b, halo_c, halo_f_one, halo_f_two, halo_k, gather_three, gather_four,
     ):
         exchange.clear()
-    flat_three[...] = jnp.zeros(flat_three.shape, jnp.float32)
-    flat_extra[...] = jnp.zeros(flat_extra.shape, jnp.float32)
+    place.greet()
+    for load in loads[4:]:
+        load.start()
     for level in range(LEVELS):
         matrices[level] = pair_matrix(depth >> level)
-    place.barrier()
-    loads[0].wait()
+    for load in loads[:4]:
+        load.wait()
+    place.await_greetings()
     halo_a.start()
 
     def spread(flat, target, count, level):
@@ -426,7 +519,8 @@
         flat[pl.ds(pl.multiple_of(plane * size, size), size), :] = value
 
     one, two, three = planes // 2, planes // 4, planes // 8
-    loads[1].wait()
+    for load in loads[4:9]:
+        load.wait()
 
     def coarse_reaction(start):
         for plane in range(4):
@@ -435,9 +529,8 @@
 
     groups(0, one, 4, coarse_reaction)
     spread(flat_zero, k_one, one, 0)
-    halo_k_one.start()
-    loads[2].wait()
-    loads[3].wait()
+    for load in loads[9:]:
+        load.wait()
 
     lanes = lane_ids((1, depth))
     patch = depth // flags.shape[2]
@@ -472,6 +565,20 @@
     add_edges(field_b, halo_a.finish(refined, 1.0 / (56.0 * midpoint)))
     halo_b.start()
 
+    for plane in range(two):
+        put(
+            flat_one, plane, one,
+            k_one[2 + 2 * plane, 8 : 8 + one, :] + k_one[3 + 2 * plane, 8 : 8 + one, :],
+        )
+    spread(flat_one, k_two, two, 1)
+    for plane in range(three):
+        put(
+            flat_two, plane, two,
+            k_two[2 + 2 * plane, 8 : 8 + two, :] + k_two[3 + 2 * plane, 8 : 8 + two, :],
+        )
+    small = paired(flat_two, matrices.at[2])
+    halo_k.start(small[0:8] + roll(small[8:16], 64, 1))
+
     def second(start):
         for index, (residual, middle) in enumerate(fine_residuals(field_b, start, 8)):
             before = field_a[start + index + 1, 8 : 8 + rows, :]
@@ -491,7 +598,6 @@
 
     groups(0, one, 4, third)
     halo_b.drain()
-    halo_k_one.drain()
     (low, high), ends = halo_c.finish(refined, 1.0 / 56.0)
     for plane in range(one):
         at = plane * rows
@@ -503,22 +609,12 @@
     spread(flat_zero, f_one, one, 0)
     halo_f_one.start()
 
-    for plane in range(two):
-        put(
-            flat_one, plane, one,
-            k_one[2 + 2 * plane, 8 : 8 + one, :] + k_one[3 + 2 * plane, 8 : 8 + one, :],
-        )
-    spread(flat_one, k_two, two, 1)
-    halo_k_two.start()
-    for plane in range(three):
-        put(
-            flat_two, plane, two,
-            k_two[2 + 2 * plane, 8 : 8 + two, :] + k_two[3 + 2 * plane, 8 : 8 + two, :],
-        )
-    small = paired(flat_two, matrices.at[2])
-    gather_k.start(small[0:8] + roll(small[8:16], 64, 1))
-    halo_k_one.finish()
+    halo_k.finish(k_three)
+    for plane in range(6):
+        flat_extra[16 * plane : 16 * plane + 16, :] = k_three[2 * plane] + k_three[2 * plane + 1]
+    k_four[...] = paired(flat_extra, matrices.at[3]).reshape(6, 8, 128)
     halo_c.drain()
+    halo_k.drain()
 
     def correct(level, f, k, e, start, count, mask):
         midpoint, factor_one, factor_two = coefficients(level)
@@ -564,59 +660,55 @@
         if level == 1:
             spread(flat, f_two, size // 2, level)
             halo_f_two.start()
-            halo_k_two.finish()
         else:
             small = paired(flat, matrices.at[level])
-            gather_f.start(small[0:8] + roll(small[8:16], 64, 1))
+            tiles_three[1, 1] = small[0:8] + roll(small[8:16], 64, 1)
+            gather_three.start()
         held[...] = e[2 : 2 + size, 8 : 8 + size, 0:extent]
         stores[level].start()
-        if level == 1:
-            halo_k_two.drain()
-            gather_k.drain()
-        else:
-            halo_f_one.drain()
-            halo_f_two.drain()
-
-    gather_k.finish(k_three)
-    for plane in range(6):
-        flat_extra[32 * plane : 32 * plane + 24, :] = (
-            k_three[4 + 2 * plane] + k_three[5 + 2 * plane]
-        )
-    k_four[...] = paired(flat_extra, matrices.at[3]).reshape(6, 16, 128)
+        exchange.drain()
 
     mask_three = in_grid(
-        8 - place.agg * three, 8 + (counts[1] - place.agg) * three, f_three.shape[1:], depth // 8
+        4 - place.agg * three, 4 + (counts[1] - place.agg) * three, f_three.shape[1:], depth // 8
     )
-    ats = {
-        plane: plane_in_grid(place.box * three + plane - 8, counts[0] * three)
-        for plane in range(3, 17)
-    }
-    gather_f.finish(f_three)
-    correct(3, f_three, k_three, e_three, 3, 14, lambda plane: mask_three * ats[plane])
-    held_three[...] = e_three[8:12, 8:12, 0 : depth // 8]
+
+    def at_three(plane):
+        return mask_three * plane_in_grid(place.box * three + plane - 4, counts[0] * three)
+
+    gather_three.arrive()
+    lay_out([[tiles_three[bx, by] for by in range(3)] for bx in range(3)], f_three)
+    correct(3, f_three, k_three, e_three, 3, 6, at_three)
+    values = left_over(f_three, k_three, e_three, 4, 4)
+    for plane in range(2):
+        flat_three[16 * plane : 16 * plane + 16, :] = values[2 * plane] + values[2 * plane + 1]
+    tiles_four[1, 1] = paired(flat_three, matrices.at[3]).reshape(2, 8, 128)
+    gather_four.start()
+    held_three[...] = e_three[4:8, 4:8, 0 : depth // 8]
     stores[3].start()
-    values = left_over(f_three, k_three, e_three, 4, 12)
-    for plane in range(6):
-        total = values[2 * plane] * (mask_three * ats[4 + 2 * plane])
-        total = total + values[2 * plane + 1] * (mask_three * ats[5 + 2 * plane])
-        flat_three[32 * plane : 32 * plane + 24, :] = total
-    f_four[...] = paired(flat_three, matrices.at[3]).reshape(6, 16, 128)
+    gather_three.drain()
 
     four = three // 2
     mask_four = in_grid(
-        4 - place.agg * four, 4 + (counts[1] - place.agg) * four, f_four.shape[1:], depth // 16
+        2 - place.agg * four, 2 + (counts[1] - place.agg) * four, f_four.shape[1:], depth // 16
     )
 
     def at_four(plane):
         return mask_four * plane_in_grid(place.box * four + plane - 2, counts[0] * four)
 
+    gather_four.arrive()
+    ids = row_ids((8, 128))
+    for plane in range(6):
+        before, own, after = (tiles_four[plane // 2, by, plane % 2] for by in range(3))
+        value = jnp.where(ids < 4, own, roll(after, 2, 0))
+        value = jnp.where(ids < 2, roll(before, -2, 0), value)
+        f_four[plane] = jnp.where(ids < 6, value, 0.0)
     correct(4, f_four, k_four, e_four, 1, 4, at_four)
-    held_four[...] = e_four[2:4, 4:6, 0 : depth // 16]
+    held_four[...] = e_four[2:4, 2:4, 0 : depth // 16]
     stores[4].start()
     for index, value in enumerate(left_over(f_four, k_four, e_four, 2, 2)):
-        held_bottom[index] = value[4:6, 0 : depth // 16]
+        held_bottom[index] = value[2:4, 0 : depth // 16]
     stores[5].start()
-    gather_f.drain()
+    gather_four.drain()
     for store in stores:
         store.wait()
 
@@ -658,12 +750,16 @@
     scratch += [vmem(planes + 2, rows + 16, depth)] * 3 + [vmem(3, 2, rows + 16, depth)]
     scratch += [pltpu.VMEM((LEVELS, 256, 128), jnp.bfloat16)]
     scratch += [vmem(one + 4, one + 16, 128)] * 3 + [vmem(two + 4, two + 16, 128)] * 3
-    scratch += [vmem(20, 24, 128)] * 3 + [vmem(6, 16, 128)] * 3
+    scratch += [vmem(12, 16, 128)] * 3 + [vmem(6, 8, 128)] * 3
     scratch += [vmem(one * rows, 128), vmem(two * one, 128), vmem(two // 2 * two, 128)]
-    scratch += [vmem(192, 128)] * 2
+    scratch += [vmem(32, 128), vmem(96, 128)]
     scratch += [vmem(3, 2, planes // 8, 8, 128)] * 2
-    scratch += [vmem(2, 2, one // 8, 8, 128)] * 2 + [vmem(2, 2, two // 8, 8, 128)] * 2
-    scratch += [vmem(7, 4, 8, 128), vmem(2, 5, 5, 8, 128)]
+    scratch += [vmem(1, 2, one // 8, 8, 128)] * 2 + [vmem(1, 2, two // 8, 8, 128)] * 2
+    k_tiles = one // 8 + two // 8 + 1
+    k_planes = 2 * (one // 8 + two // 8) + 1
+    scratch += [vmem(5, 4, 8, 128), vmem(2, k_tiles, 8, 128), vmem(2, k_planes, 8, 128)]
+    scratch += [vmem(2, k_tiles, 8, 128), vmem(4, k_tiles, 8, 128), vmem(2, k_planes, 8, 128)]
+    scratch += [vmem(3, 3, 8, 128), vmem(3, 3, 2, 8, 128)]
     outs = [jax.ShapeDtypeStruct(source.shape, f32)]
     for level in range(1, LEVELS + 1):
         outs.append(
@@ -671,8 +767,8 @@
         )
     outs.append(outs[-1])
     scratch += [vmem(*out.shape) for out in outs[1:]]
-    scratch += [pltpu.SemaphoreType.DMA((7, 8))] * 2 + [pltpu.SemaphoreType.DMA((2, 24))] * 2
-    scratch += [pltpu.SemaphoreType.DMA((10,))]
+    scratch += [pltpu.SemaphoreType.DMA((8, 8))] * 2
+    scratch += [pltpu.SemaphoreType.DMA((19,))]
     anywhere = pl.BlockSpec(memory_space=pl.ANY)
     results = pl.pallas_call(
         functools.partial(kernel, counts),

time: 33.7 us -> 34.6 us (1.027)
  Pallas kernels: 32.7 us -> 33.8 us
    pallas_call x1, Pallas kernels: 30.7 us -> 31.8 us  [per_device(): pl.pallas_call(functools.partial(kernel, counts), out_shape=outs, in_spec...]
where the time goes in v4:
time: 34.6 us; the launch traced here: 34.4 us
  Pallas kernels  33.8 us (98%)
  between operations  0.64 us (2%)
    pallas_call x1, Pallas kernels, per_device(): pl.pallas_call(functools.partial(kernel, counts), out_shape=outs, in_spec...  31.8 us
    pallas_call x1, Pallas kernels, per_device(): pl.pallas_call(hand_on, out_shape=outs, in_specs=[anywhere] * 6, out_spec...  1.99 us

profile of v4, /device:TPU:1, one launch (start us, length us, event | category | flops | bytes accessed | tf_op | source)
XLA Modules:
  0.0 34.4 jit_solution(9817272869988866640)
XLA Ops:
  0.6 31.8 %shard_map.91 = (f32[32,32,128]{2,1,0:T(8,128)}, f32[16,16,64]{2,1,0:T(8,128)}, f32[8,8,32]{2,1,0:T(8,128)}, f32[4,4,16]{2,1,0:T(4,128)}, f32[2,2,8]{2,1,0:T(2,128)}, /*index=5*/f32[2,2,8]{2,1,0:T(2,128)}) custom-call(s32[1,1,4]{2,1,0:T(1,128)} %flags_in.1, f32[32,32,128]{2,1,0:T(8,128)} %source_in.1, f32[32,32,128]{2,1,0:T(8,128)} %guess_in.1, ...), custom_call_target="tpu_custom_call" | custom-call | tf_op jit(solution)/shard_map/pallas_call | solution.py:773
  32.4 2.0 %shard_map.92 = (f32[32,32,128]{2,1,0:T(8,128)}, f32[16,16,64]{2,1,0:T(8,128)}, f32[8,8,32]{2,1,0:T(8,128)}, f32[4,4,16]{2,1,0:T(4,128)}, f32[2,2,8]{2,1,0:T(2,128)}, /*index=5*/f32[2,2,8]{2,1,0:T(2,128)}) custom-call(f32[32,32,128]{2,1,0:T(8,128)} %get-tuple-element.12.refs_0_, f32[16,16,64]{2,1,0:T(8,128)} %get-tuple-element.13.refs_1_, ...), custom_call_target="tpu_custom_call" | custom-call | tf_op jit(solution)/shard_map/pallas_call | solution.py:784

commit v5 on v4

--- a/solution.py
+++ b/solution.py
@@ -257,8 +257,8 @@
             device_id_type=MESH,
         )
 
-    def start(self, tile):
-        self.tile = tile
+    def start(self, tiles):
+        self.tiles = tiles
         at = 0
         for block in self.fields:
             size = (block.shape[0] - 4) // 8
@@ -276,11 +276,12 @@
                 at += size
         for ref in (self.packs, self.ends):
             for index in range(2):
-                ref[index, ref.shape[1] - 1] = tile
+                for where, tile in enumerate(tiles):
+                    ref[index, ref.shape[1] - 2 + where] = tile
         for number, (dx, dy) in enumerate(NEAR):
             pl.when(self.place.has(dx, dy))(lambda n=number: self.copy(n).start())
 
-    def finish(self, third):
+    def finish(self, second):
         self.arrive()
         at, end = 0, 0
         for block in self.fields:
@@ -300,26 +301,35 @@
                     block[plane, 8 : 8 + rows, :] = value
             at += count
             end += 2 * size
-        around = [
-            [self.corners[0, at], self.outer[0, end], self.corners[1, at]],
-            [self.sides[0, at], self.tile, self.sides[1, at]],
-            [self.corners[2, at], self.outer[1, end], self.corners[3, at]],
-        ]
-        lay_out(around, third)
+        around = []
+        for part in range(2):
+            side, last = at + part, end + part
+            around.append(
+                [
+                    [self.corners[0, side], self.outer[0, last], self.corners[1, side]],
+                    [self.sides[0, side], self.tiles[part], self.sides[1, side]],
+                    [self.corners[2, side], self.outer[1, last], self.corners[3, side]],
+                ]
+            )
+        lay_out(around, second)
+
+
+def fold(values):
+    tiles = []
+    for part in range(2):
+        planes = [roll(values[32 * part + 8 * at : 32 * part + 8 * at + 8], 32 * at, 1) for at in range(4)]
+        tiles.append((planes[0] + planes[1]) + (planes[2] + planes[3]))
+    return tiles
 
 
 def lay_out(around, field):
-    rows, lanes = row_ids((8, 128)), lane_ids((8, 128))
+    lanes = lane_ids((8, 128))
     for bx in range(3):
-        for index in range(4):
-            values = []
-            for by in range(3):
-                value = roll(around[bx][by], 4 * (by % 2) - 4 * (index % 2), 0)
-                values.append(roll(value, 64, 1) if index >= 2 else value)
-            head = jnp.where(rows < 4, values[0], values[1])
-            tail = jnp.where(rows < 4, values[2], 0.0)
-            field[4 * bx + index, 0:8, :] = jnp.where(lanes < 64, head, 0.0)
-            field[4 * bx + index, 8:16, :] = jnp.where(lanes < 64, tail, 0.0)
+        for by in range(3):
+            for index in range(8):
+                value = roll(around[index // 4][bx][by], -32 * (index % 4), 1)
+                value = jnp.where(lanes < 32, value, 0.0)
+                field[8 * bx + index, 8 * by : 8 * by + 8, :] = value
 
 
 class Gather(Halo):
@@ -446,8 +456,8 @@
     f_one, k_one, e_one, f_two, k_two, e_two,
     f_three, k_three, e_three, f_four, k_four, e_four,
     flat_zero, flat_one, flat_two, flat_three, flat_extra,
-    packs_zero, sides_zero, packs_one, sides_one, packs_two, sides_two, corners,
-    k_packs, k_ends, k_sides, k_corners, k_outer, tiles_three, tiles_four, held_one, held_two, held_three, held_four, held_bottom,
+    packs_zero, sides_zero, packs_one, sides_one, corners,
+    k_packs, k_ends, k_sides, k_corners, k_outer, tiles_two, tiles_four, held_one, held_two, held_three, held_four, held_bottom,
     near_send, near_recv, local,
 ):
     place = Place(counts)
@@ -467,13 +477,12 @@
         for index, block in enumerate((field_a, field_b, field_c))
     )
     halo_f_one = halo(3, f_one, 2, packs_one, sides_one, 0)
-    halo_f_two = halo(4, f_two, 2, packs_two, sides_two, 0)
+    gather_two = Gather(place, tiles_two, near_send.at[4], near_recv.at[4])
     halo_k = Coefficients(
-        place, (k_one, k_two), k_packs, k_ends, k_sides, k_corners, k_outer,
+        place, (k_one,), k_packs, k_ends, k_sides, k_corners, k_outer,
         near_send.at[5], near_recv.at[5],
     )
-    gather_three = Gather(place, tiles_three, near_send.at[6], near_recv.at[6])
-    gather_four = Gather(place, tiles_four, near_send.at[7], near_recv.at[7])
+    gather_four = Gather(place, tiles_four, near_send.at[6], near_recv.at[6])
     own_a = field_a.at[1 : 1 + planes, 8 : 8 + rows]
     own_c = field_c.at[1 : 1 + planes, 8 : 8 + rows]
     quarter = planes // 4
@@ -498,10 +507,12 @@
     for load in loads[:4]:
         load.start()
     for exchange in (
-        halo_a, halo_b, halo_c, halo_f_one, halo_f_two, halo_k, gather_three, gather_four,
+        halo_a, halo_b, halo_c, halo_f_one, gather_two, halo_k, gather_four,
     ):
         exchange.clear()
     place.greet()
+    flat_two[...] = jnp.zeros(flat_two.shape, jnp.float32)
+    flat_extra[...] = jnp.zeros(flat_extra.shape, jnp.float32)
     for load in loads[4:]:
         load.start()
     for level in range(LEVELS):
@@ -570,14 +581,8 @@
             flat_one, plane, one,
             k_one[2 + 2 * plane, 8 : 8 + one, :] + k_one[3 + 2 * plane, 8 : 8 + one, :],
         )
-    spread(flat_one, k_two, two, 1)
-    for plane in range(three):
-        put(
-            flat_two, plane, two,
-            k_two[2 + 2 * plane, 8 : 8 + two, :] + k_two[3 + 2 * plane, 8 : 8 + two, :],
-        )
-    small = paired(flat_two, matrices.at[2])
-    halo_k.start(small[0:8] + roll(small[8:16], 64, 1))
+    k_tiles = fold(paired(flat_one, matrices.at[1]))
+    halo_k.start(k_tiles)
 
     def second(start):
         for index, (residual, middle) in enumerate(fine_residuals(field_b, start, 8)):
@@ -609,10 +614,13 @@
     spread(flat_zero, f_one, one, 0)
     halo_f_one.start()
 
-    halo_k.finish(k_three)
+    halo_k.finish(k_two)
+    for plane in range(12):
+        flat_extra[32 * plane : 32 * plane + 24, :] = k_two[2 * plane] + k_two[2 * plane + 1]
+    k_three[...] = paired(flat_extra, matrices.at[2]).reshape(12, 16, 128)
     for plane in range(6):
-        flat_extra[16 * plane : 16 * plane + 16, :] = k_three[2 * plane] + k_three[2 * plane + 1]
-    k_four[...] = paired(flat_extra, matrices.at[3]).reshape(6, 8, 128)
+        flat_three[16 * plane : 16 * plane + 16, :] = k_three[2 * plane] + k_three[2 * plane + 1]
+    k_four[...] = paired(flat_three, matrices.at[3]).reshape(6, 8, 128)
     halo_c.drain()
     halo_k.drain()
 
@@ -632,41 +640,52 @@
             for index, (total, middle) in enumerate(weighted(e, start, count, False))
         ]
 
-    for level, f, k, e, exchange, held, flat, size, spans in (
-        (1, f_one, k_one, e_one, halo_f_one, held_one, flat_one, one, (6, 4)),
-        (2, f_two, k_two, e_two, halo_f_two, held_two, flat_two, two, (10, 4)),
-    ):
-        extent = depth >> level
-        exchange.finish()
-        row_mask = in_grid(
-            8 - place.agg * size, 8 + (counts[1] - place.agg) * size, f.shape[1:], extent
-        )
-
-        def mask(plane, size=size, row_mask=row_mask):
-            return row_mask * plane_in_grid(place.box * size + plane - 2, counts[0] * size)
-
-        def ahead(start, level=level, f=f, k=k, e=e, span=spans[0], mask=mask):
-            correct(level, f, k, e, start, span, mask)
-
-        groups(1, size + 2, spans[0], ahead)
-
-        def remainder(start, f=f, k=k, e=e, size=size, flat=flat, span=spans[1]):
-            values = left_over(f, k, e, 2 * start + 2, 2 * span)
-            for index in range(span):
-                total = values[2 * index] + values[2 * index + 1]
-                put(flat, start + index, size, total[8 : 8 + size])
-
-        groups(0, size // 2, spans[1], remainder)
-        if level == 1:
-            spread(flat, f_two, size // 2, level)
-            halo_f_two.start()
-        else:
-            small = paired(flat, matrices.at[level])
-            tiles_three[1, 1] = small[0:8] + roll(small[8:16], 64, 1)
-            gather_three.start()
-        held[...] = e[2 : 2 + size, 8 : 8 + size, 0:extent]
-        stores[level].start()
-        exchange.drain()
+    halo_f_one.finish()
+    mask_one = in_grid(
+        8 - place.agg * one, 8 + (counts[1] - place.agg) * one, f_one.shape[1:], depth // 2
+    )
+
+    def at_one(plane):
+        return mask_one * plane_in_grid(place.box * one + plane - 2, counts[0] * one)
+
+    groups(1, one + 2, 6, lambda start: correct(1, f_one, k_one, e_one, start, 6, at_one))
+
+    def remainder(start):
+        values = left_over(f_one, k_one, e_one, 2 * start + 2, 8)
+        for index in range(4):
+            total = values[2 * index] + values[2 * index + 1]
+            put(flat_one, start + index, one, total[8 : 8 + one])
+
+    groups(0, two, 4, remainder)
+    for part, tile in enumerate(fold(paired(flat_one, matrices.at[1]))):
+        tiles_two[1, 1, part] = tile
+    gather_two.start()
+    held_one[...] = e_one[2 : 2 + one, 8 : 8 + one, 0 : depth // 2]
+    stores[1].start()
+    halo_f_one.drain()
+
+    mask_two = in_grid(
+        8 - place.agg * two, 8 + (counts[1] - place.agg) * two, f_two.shape[1:], depth // 4
+    )
+
+    def at_two(plane):
+        return mask_two * plane_in_grid(place.box * two + plane - 8, counts[0] * two)
+
+    gather_two.arrive()
+    lay_out(
+        [
+            [[tiles_two[bx, by, part] for by in range(3)] for bx in range(3)]
+            for part in range(2)
+        ],
+        f_two,
+    )
+    correct(2, f_two, k_two, e_two, 3, 18, at_two)
+    values = left_over(f_two, k_two, e_two, 4, 16)
+    for plane in range(8):
+        total = values[2 * plane] * at_two(4 + 2 * plane)
+        total = total + values[2 * plane + 1] * at_two(5 + 2 * plane)
+        flat_two[32 * plane : 32 * plane + 24, :] = total
+    f_three[2:10] = paired(flat_two, matrices.at[2]).reshape(8, 16, 128)
 
     mask_three = in_grid(
         4 - place.agg * three, 4 + (counts[1] - place.agg) * three, f_three.shape[1:], depth // 8
@@ -675,17 +694,17 @@
     def at_three(plane):
         return mask_three * plane_in_grid(place.box * three + plane - 4, counts[0] * three)
 
-    gather_three.arrive()
-    lay_out([[tiles_three[bx, by] for by in range(3)] for bx in range(3)], f_three)
     correct(3, f_three, k_three, e_three, 3, 6, at_three)
     values = left_over(f_three, k_three, e_three, 4, 4)
     for plane in range(2):
         flat_three[16 * plane : 16 * plane + 16, :] = values[2 * plane] + values[2 * plane + 1]
-    tiles_four[1, 1] = paired(flat_three, matrices.at[3]).reshape(2, 8, 128)
+    tiles_four[1, 1] = paired(flat_three.at[0:32], matrices.at[3]).reshape(2, 8, 128)
     gather_four.start()
     held_three[...] = e_three[4:8, 4:8, 0 : depth // 8]
     stores[3].start()
-    gather_three.drain()
+    held_two[...] = e_two[8 : 8 + two, 8 : 8 + two, 0 : depth // 4]
+    stores[2].start()
+    gather_two.drain()
 
     four = three // 2
     mask_four = in_grid(
@@ -749,17 +768,17 @@
     scratch = [pltpu.VMEM(flags.shape, jnp.int32)] + [vmem(planes, rows, depth)] * 2
     scratch += [vmem(planes + 2, rows + 16, depth)] * 3 + [vmem(3, 2, rows + 16, depth)]
     scratch += [pltpu.VMEM((LEVELS, 256, 128), jnp.bfloat16)]
-    scratch += [vmem(one + 4, one + 16, 128)] * 3 + [vmem(two + 4, two + 16, 128)] * 3
+    scratch += [vmem(one + 4, one + 16, 128)] * 3 + [vmem(24, 24, 128)] * 3
     scratch += [vmem(12, 16, 128)] * 3 + [vmem(6, 8, 128)] * 3
-    scratch += [vmem(one * rows, 128), vmem(two * one, 128), vmem(two // 2 * two, 128)]
-    scratch += [vmem(32, 128), vmem(96, 128)]
+    scratch += [vmem(one * rows, 128), vmem(two * one, 128), vmem(256, 128)]
+    scratch += [vmem(96, 128), vmem(384, 128)]
     scratch += [vmem(3, 2, planes // 8, 8, 128)] * 2
-    scratch += [vmem(1, 2, one // 8, 8, 128)] * 2 + [vmem(1, 2, two // 8, 8, 128)] * 2
-    k_tiles = one // 8 + two // 8 + 1
-    k_planes = 2 * (one // 8 + two // 8) + 1
-    scratch += [vmem(5, 4, 8, 128), vmem(2, k_tiles, 8, 128), vmem(2, k_planes, 8, 128)]
+    scratch += [vmem(1, 2, one // 8, 8, 128)] * 2
+    k_tiles = one // 8 + 2
+    k_planes = 2 * (one // 8) + 2
+    scratch += [vmem(4, 4, 8, 128), vmem(2, k_tiles, 8, 128), vmem(2, k_planes, 8, 128)]
     scratch += [vmem(2, k_tiles, 8, 128), vmem(4, k_tiles, 8, 128), vmem(2, k_planes, 8, 128)]
-    scratch += [vmem(3, 3, 8, 128), vmem(3, 3, 2, 8, 128)]
+    scratch += [vmem(3, 3, 2, 8, 128)] * 2
     outs = [jax.ShapeDtypeStruct(source.shape, f32)]
     for level in range(1, LEVELS + 1):
         outs.append(
@@ -767,7 +786,7 @@
         )
     outs.append(outs[-1])
     scratch += [vmem(*out.shape) for out in outs[1:]]
-    scratch += [pltpu.SemaphoreType.DMA((8, 8))] * 2
+    scratch += [pltpu.SemaphoreType.DMA((7, 8))] * 2
     scratch += [pltpu.SemaphoreType.DMA((19,))]
     anywhere = pl.BlockSpec(memory_space=pl.ANY)
     results = pl.pallas_call(

time: 34.6 us -> 31.2 us (0.902)
  Pallas kernels: 33.8 us -> 30.4 us
    pallas_call x1, Pallas kernels: 31.8 us -> 28.5 us  [per_device(): pl.pallas_call(functools.partial(kernel, counts), out_shape=outs, in_spec...]
where the time goes in v5:
time: 31.2 us; the launch traced here: 31.1 us
  Pallas kernels  30.4 us (97%)
  between operations  0.64 us (2%)
    pallas_call x1, Pallas kernels, per_device(): pl.pallas_call(functools.partial(kernel, counts), out_shape=outs, in_spec...  28.5 us
    pallas_call x1, Pallas kernels, per_device(): pl.pallas_call(hand_on, out_shape=outs, in_specs=[anywhere] * 6, out_spec...  1.99 us

profile of v5, /device:TPU:1, one launch (start us, length us, event | category | flops | bytes accessed | tf_op | source)
XLA Modules:
  0.0 31.1 jit_solution(4892013949601356354)
XLA Ops:
  0.6 28.5 %shard_map.91 = (f32[32,32,128]{2,1,0:T(8,128)}, f32[16,16,64]{2,1,0:T(8,128)}, f32[8,8,32]{2,1,0:T(8,128)}, f32[4,4,16]{2,1,0:T(4,128)}, f32[2,2,8]{2,1,0:T(2,128)}, /*index=5*/f32[2,2,8]{2,1,0:T(2,128)}) custom-call(s32[1,1,4]{2,1,0:T(1,128)} %flags_in.1, f32[32,32,128]{2,1,0:T(8,128)} %source_in.1, f32[32,32,128]{2,1,0:T(8,128)} %guess_in.1, ...), custom_call_target="tpu_custom_call" | custom-call | tf_op jit(solution)/shard_map/pallas_call | solution.py:792
  29.1 2.0 %shard_map.92 = (f32[32,32,128]{2,1,0:T(8,128)}, f32[16,16,64]{2,1,0:T(8,128)}, f32[8,8,32]{2,1,0:T(8,128)}, f32[4,4,16]{2,1,0:T(4,128)}, f32[2,2,8]{2,1,0:T(2,128)}, /*index=5*/f32[2,2,8]{2,1,0:T(2,128)}) custom-call(f32[32,32,128]{2,1,0:T(8,128)} %get-tuple-element.12.refs_0_, f32[16,16,64]{2,1,0:T(8,128)} %get-tuple-element.13.refs_1_, ...), custom_call_target="tpu_custom_call" | custom-call | tf_op jit(solution)/shard_map/pallas_call | solution.py:803

commit v6 on v5

--- a/solution.py
+++ b/solution.py
@@ -569,10 +569,10 @@
         block[planes, 8 : 8 + rows, :] += ends[1]
 
     def first(start):
-        for index, (residual, middle) in enumerate(fine_residuals(field_a, start, 8)):
+        for index, (residual, middle) in enumerate(fine_residuals(field_a, start, 16)):
             field_b[start + index + 1, 8 : 8 + rows, :] = middle + residual * (1.0 / midpoint)
 
-    groups(0, planes, 8, first)
+    groups(0, planes, 16, first)
     add_edges(field_b, halo_a.finish(refined, 1.0 / (56.0 * midpoint)))
     halo_b.start()
 
@@ -585,23 +585,23 @@
     halo_k.start(k_tiles)
 
     def second(start):
-        for index, (residual, middle) in enumerate(fine_residuals(field_b, start, 8)):
+        for index, (residual, middle) in enumerate(fine_residuals(field_b, start, 16)):
             before = field_a[start + index + 1, 8 : 8 + rows, :]
             step = factor_one * (middle - before) + factor_two * residual
             field_c[start + index + 1, 8 : 8 + rows, :] = middle + step
 
-    groups(0, planes, 8, second)
+    groups(0, planes, 16, second)
     halo_a.drain()
     add_edges(field_c, halo_b.finish(refined, factor_two / 56.0))
     halo_c.start()
     stores[0].start()
 
     def third(start):
-        values = fine_residuals(field_c, 2 * start, 8)
-        for index in range(4):
+        values = fine_residuals(field_c, 2 * start, 16)
+        for index in range(8):
             put(flat_zero, start + index, rows, values[2 * index][0] + values[2 * index + 1][0])
 
-    groups(0, one, 4, third)
+    groups(0, one, 8, third)
     halo_b.drain()
     (low, high), ends = halo_c.finish(refined, 1.0 / 56.0)
     for plane in range(one):
@@ -648,15 +648,15 @@
     def at_one(plane):
         return mask_one * plane_in_grid(place.box * one + plane - 2, counts[0] * one)
 
-    groups(1, one + 2, 6, lambda start: correct(1, f_one, k_one, e_one, start, 6, at_one))
+    groups(1, one + 2, 18, lambda start: correct(1, f_one, k_one, e_one, start, 18, at_one))
 
     def remainder(start):
-        values = left_over(f_one, k_one, e_one, 2 * start + 2, 8)
-        for index in range(4):
+        values = left_over(f_one, k_one, e_one, 2 * start + 2, 16)
+        for index in range(8):
             total = values[2 * index] + values[2 * index + 1]
             put(flat_one, start + index, one, total[8 : 8 + one])
 
-    groups(0, two, 4, remainder)
+    groups(0, two, 8, remainder)
     for part, tile in enumerate(fold(paired(flat_one, matrices.at[1]))):
         tiles_two[1, 1, part] = tile
     gather_two.start()

time: 31.2 us -> 30.9 us (level)
    pallas_call x1, Pallas kernels: 28.5 us -> 28.1 us  [per_device(): pl.pallas_call(functools.partial(kernel, counts), out_shape=outs, in_spec...]
where the time goes in v6:
time: 30.9 us; the launch traced here: 30.7 us
  Pallas kernels  30.1 us (97%)
  between operations  0.64 us (2%)
    pallas_call x1, Pallas kernels, per_device(): pl.pallas_call(functools.partial(kernel, counts), out_shape=outs, in_spec...  28.1 us
    pallas_call x1, Pallas kernels, per_device(): pl.pallas_call(hand_on, out_shape=outs, in_specs=[anywhere] * 6, out_spec...  1.99 us

profile of v6, /device:TPU:1, one launch (start us, length us, event | category | flops | bytes accessed | tf_op | source)
XLA Modules:
  0.0 30.7 jit_solution(5805554724814603352)
XLA Ops:
  0.6 28.1 %shard_map.91 = (f32[32,32,128]{2,1,0:T(8,128)}, f32[16,16,64]{2,1,0:T(8,128)}, f32[8,8,32]{2,1,0:T(8,128)}, f32[4,4,16]{2,1,0:T(4,128)}, f32[2,2,8]{2,1,0:T(2,128)}, /*index=5*/f32[2,2,8]{2,1,0:T(2,128)}) custom-call(s32[1,1,4]{2,1,0:T(1,128)} %flags_in.1, f32[32,32,128]{2,1,0:T(8,128)} %source_in.1, f32[32,32,128]{2,1,0:T(8,128)} %guess_in.1, ...), custom_call_target="tpu_custom_call" | custom-call | tf_op jit(solution)/shard_map/pallas_call | solution.py:792
  28.7 2.0 %shard_map.92 = (f32[32,32,128]{2,1,0:T(8,128)}, f32[16,16,64]{2,1,0:T(8,128)}, f32[8,8,32]{2,1,0:T(8,128)}, f32[4,4,16]{2,1,0:T(4,128)}, f32[2,2,8]{2,1,0:T(2,128)}, /*index=5*/f32[2,2,8]{2,1,0:T(2,128)}) custom-call(f32[32,32,128]{2,1,0:T(8,128)} %get-tuple-element.12.refs_0_, f32[16,16,64]{2,1,0:T(8,128)} %get-tuple-element.13.refs_1_, ...), custom_call_target="tpu_custom_call" | custom-call | tf_op jit(solution)/shard_map/pallas_call | solution.py:803
